TPU v7x, 128 devices: a whole 4x4x4 slice. The times are simulated.
128 devices in a mesh: aa: 8 (over x_hi, z), ba: 16 (over x_lo, y, core).
Axes of the slice: x: 4 (x_hi: 2, x_lo: 2; x = x_hi * 2 + x_lo), y: 4, z: 4, core: 2. Of those that a mesh axis runs over, the one named last changes fastest.
Arguments:
- feats: bfloat16 [8, 64, 128, 256], P('aa', 'ba'), may hold values from -6 to 6
- conv_one: bfloat16 [3, 3, 3, 256, 256], replicated, may hold values from -0.078125 to 0.078125
- bias_one: float32 [256], replicated, may hold values from -3 to 3
- conv_two: bfloat16 [3, 3, 3, 256, 256], replicated, may hold values from -0.078125 to 0.078125
- bias_two: float32 [256], replicated, may hold values from -3 to 3
- patch_weight: bfloat16 [2, 2, 256, 128], replicated, may hold values from -0.1875 to 0.1875
- patch_bias: float32 [128], replicated, may hold values from -3 to 3
- embed_weight: bfloat16 [128, 2048], replicated, may hold values from -0.5 to 0.5
- embed_bias: float32 [2048], replicated, may hold values from -6 to 6
- norm_gain: float32 [2048], replicated, may hold values from 0.1 to 1.9
- w_query: bfloat16 [2048, 2048], P(None, 'ba'), may hold values from -2 to 2
- w_key: bfloat16 [2048, 2048], P(None, 'ba'), may hold values from -2 to 2
- w_value: bfloat16 [2048, 2048], P(None, 'ba'), may hold values from -0.125 to 0.125
- w_velocity: bfloat16 [2048, 128], P('ba'), may hold values from -0.5 to 0.5
Outputs:
- velocity: float32 [16384, 128], P(('aa', 'ba'))
All inputs are finite; a program needn't handle non-finite values.
Results may differ from a plain program's by a relative error of at most 0.035.
Values may be sent and summed in bfloat16 or wider, within the bound.
No kernel may reach another device: no remote copies, remote signals or barrier semaphores. Data moves between devices by JAX's collectives and lax.ppermute only.
A program may use at most 128 MiB of HBM per device.

v0:
```python
import math

import jax
import jax.numpy as jnp
from jax import lax
from jax.sharding import PartitionSpec as P

HEAD_DIM = 64


def with_halo(cells, sides, width):
    for axis, dim in sides:
        count = lax.axis_size(axis)
        ends = count - 1
        head = lax.slice_in_dim(cells, 0, width, axis=dim)
        tail = lax.slice_in_dim(cells, cells.shape[dim] - width, cells.shape[dim], axis=dim)
        cells = jnp.concatenate(
            [
                lax.ppermute(tail, axis, [(i, (i + 1) % count) for i in range(ends)]),
                cells,
                lax.ppermute(head, axis, [((i + 1) % count, i) for i in range(ends)]),
            ],
            axis=dim,
        )
    return cells


def side_by_side(arrays, axis, dim, along):
    both = jnp.concatenate(arrays, axis=along)
    filled, at, gathered = (lax.all_gather(both, axis, axis=dim, tiled=True), 0, [])
    for a in arrays:
        gathered.append(lax.slice_in_dim(filled, at, at + a.shape[along], axis=along))
        at += a.shape[along]
    return tuple(gathered)


def in_order(parts, dim):
    dims = list(parts.shape[1:])
    dims[dim] *= parts.shape[0]
    return jnp.moveaxis(parts, 0, dim).reshape(dims)


def copy_for_each(x, axis):
    copies = jnp.broadcast_to(x, (lax.axis_size(axis), *x.shape))
    return lax.all_to_all(copies, axis, split_axis=0, concat_axis=0, tiled=True)


def gather_directly(x, axis, dim):
    return in_order(copy_for_each(x, axis), dim)


def cut_along(x, dim, peers):
    before, after = (x.shape[:dim], x.shape[dim + 1 :])
    return jnp.moveaxis(x.reshape(*before, peers, -1, *after), dim, 0)


def sent_and_summed(x, axis, dim):
    peers = lax.axis_size(axis)
    parts = lax.all_to_all(cut_along(x, dim, peers), axis, 0, 0, tiled=True)
    return jnp.sum(parts.astype(jnp.float32), axis=0)


def convolve(field, kernel, bias):
    frames, rows, width, chans = field.shape
    padded = with_halo(field, (("aa", 0), ("ba", 1)), 1)
    padded = jnp.pad(padded, ((0, 0), (0, 0), (1, 1), (0, 0)))
    total = jnp.zeros((frames * rows * width, kernel.shape[-1]), jnp.float32)
    for shift_t in range(3):
        for shift_r in range(3):
            window = padded[shift_t : shift_t + frames, shift_r : shift_r + rows]
            stacked = jnp.concatenate(
                [window[:, :, shift_w : shift_w + width] for shift_w in range(3)], axis=-1
            )
            total = total + jnp.dot(
                stacked.reshape(-1, 3 * chans),
                kernel[shift_t, shift_r].reshape(3 * chans, -1),
                preferred_element_type=jnp.float32,
            )
    return (total + bias).reshape(frames, rows, width, -1)


def patchify(field, weight, bias):
    frames, rows, width, chans = field.shape
    blocks = (
        field.reshape(frames, rows // 2, 2, width // 2, 2, chans)
        .transpose(0, 1, 3, 2, 4, 5)
        .reshape(-1, 4 * chans)
    )
    return (
        jnp.dot(blocks, weight.reshape(4 * chans, -1), preferred_element_type=jnp.float32) + bias
    ).astype(jnp.bfloat16)


def normalize(latent_rows, embed_weight, embed_bias, norm_gain):
    hidden = jnp.dot(latent_rows, embed_weight, preferred_element_type=jnp.float32) + embed_bias
    center = hidden - hidden.mean(-1, keepdims=True)
    spread = (center * center).mean(-1, keepdims=True)
    return (center * lax.rsqrt(spread + 1e-05) * norm_gain).astype(jnp.bfloat16)


def attend(queries, keys, values):
    rows, width = queries.shape
    heads = width // HEAD_DIM
    scale = HEAD_DIM ** (-0.5)
    query_heads = queries.reshape(rows, heads, HEAD_DIM)
    start_state = (
        jnp.full((heads, rows), -jnp.inf, jnp.float32),
        jnp.zeros((heads, rows), jnp.float32),
        jnp.zeros((rows, heads, HEAD_DIM), jnp.float32),
    )
    key_rows, value_rows = side_by_side((keys, values), "aa", 0, 1)
    count = key_rows.shape[0]
    block = math.gcd(count, 1024)

    def one_step(index, state):
        best, denom, accum = state
        key_block = lax.dynamic_slice_in_dim(key_rows, index * block, block, 0).reshape(
            block, heads, HEAD_DIM
        )
        value_block = lax.dynamic_slice_in_dim(value_rows, index * block, block, 0).reshape(
            block, heads, HEAD_DIM
        )
        scores = (
            jnp.einsum("qhd,khd->hqk", query_heads, key_block, preferred_element_type=jnp.float32)
            * scale
        )
        peak = jnp.maximum(best, scores.max(-1))
        probs = jnp.exp(scores - peak[..., None])
        fade = jnp.exp(best - peak)
        denom = denom * fade + probs.sum(-1)
        accum = accum * fade.T[..., None] + jnp.einsum(
            "hqk,khd->qhd",
            probs.astype(jnp.bfloat16),
            value_block,
            preferred_element_type=jnp.float32,
        )
        return (peak, denom, accum)

    best, denom, accum = lax.fori_loop(0, count // block, one_step, start_state)
    return (accum / denom.T[..., None]).reshape(rows, width).astype(jnp.bfloat16)


def on_device(
    feats,
    conv_one,
    bias_one,
    conv_two,
    bias_two,
    patch_weight,
    patch_bias,
    embed_weight,
    embed_bias,
    norm_gain,
    w_query,
    w_key,
    w_value,
    w_velocity,
):
    first = jax.nn.gelu(convolve(feats, conv_one, bias_one), approximate=False).astype(jnp.bfloat16)
    second = (
        first.astype(jnp.float32)
        + jax.nn.gelu(convolve(first, conv_two, bias_two), approximate=False)
    ).astype(jnp.bfloat16)
    latents = patchify(second, patch_weight, patch_bias)
    width = w_query.shape[1]
    w_joined = jnp.concatenate([w_query, w_key, w_value], axis=1)
    joined = jnp.dot(
        normalize(gather_directly(latents, "ba", 0), embed_weight, embed_bias, norm_gain),
        w_joined,
        preferred_element_type=jnp.float32,
    ).astype(jnp.bfloat16)
    attended = attend(joined[:, :width], joined[:, width : 2 * width], joined[:, 2 * width :])
    return sent_and_summed(
        jnp.dot(attended, w_velocity, preferred_element_type=jnp.float32).astype(jnp.bfloat16),
        "ba",
        0,
    )


def solution(mesh):
    return jax.shard_map(
        on_device,
        mesh=mesh,
        in_specs=(
            P("aa", "ba", None, None),
            P(),
            P(),
            P(),
            P(),
            P(),
            P(),
            P(),
            P(),
            P(),
            P(None, "ba"),
            P(None, "ba"),
            P(None, "ba"),
            P("ba", None),
        ),
        out_specs=P(("aa", "ba"), None),
        check_vma=False,
    )
```

profile of v0, /device:TPU:1, one launch (start us, length us, event | category | flops | bytes accessed | tf_op | source)
XLA Modules:
  0.0 665.3 jit_solution(9328303637522487848)
XLA Ops:
  80.1 16.8 %all_to_all.10 = bf16[16,128,128]{2,1,0:T(8,128)(2,1)S(1)} all-to-all(bf16[16,128,128]{2,1,0:T(8,128)(2,1)S(1)} %broadcast_in_dim.29), channel_id=1, replica_groups=mesh['aa'=8,'ba'=16] {'ba'}, dimensions={0} | all-to-all | bytes 1048576 | tf_op jit(solution)/shard_map/all_to_all | solution.py:45
  104.0 8.2 %multiply_reduce_fusion = f32[2048]{0:T(1024)S(1)} fusion(f32[2048,2048]{0,1:T(8,128)} %get-tuple-element.254, f32[2048]{0:T(1024)S(1)} %broadcast_multiply_fusion.2, f32[2048]{0:T(1024)S(1)} %copy-done.13), kind=kLoop, calls=%fused_computation.19 | loop fusion | flops 16775168 | bytes 16801792 | tf_op jit(solution)/shard_map/reduce_sum | solution.py:97
  112.2 8.9 %fusion.16 = bf16[2048,384]{0,1:T(8,128)(2,1)S(1)} fusion(f32[2048,2048]{0,1:T(8,128)} %get-tuple-element.254, f32[2048]{0:T(1024)S(1)} %copy-done.20, f32[2048]{0:T(1024)S(1)} %add_rsqrt_fusion, f32[2048]{0:T(1024)S(1)} %broadcast_multiply_fusion.2, f32[2048]{0:T(1024)S(1)} %copy-done.13, bf16[2048,128]{1,0:T(8,128)(2,1)S(1)} %copy-done.17, ...), kind=kOutput, calls=%fused_computation.24 | convolution fusion | flops 3247702016 | bytes 19955712 | tf_op jit(solution)/shard_map/dot_general | solution.py:167
  122.7 109.7 %all-gather.2.cloned.1.call-done = bf16[16384,256]{0,1:T(8,128)(2,1)} async-done(((bf16[2048,256]{0,1:T(8,128)(2,1)}), bf16[16384,256]{0,1:T(8,128)(2,1)}) %all-gather.2.cloned.1.call-update) | async-done | bytes 8388624 | tf_op jit(solution)/shard_map/all_gather | solution.py:30
  238.3 403.3 %while.18 = (s32[]{:T(128)}, f32[2,2048]{1,0:T(2,128)S(1)}, f32[2,2048]{1,0:T(2,128)S(1)}, f32[2048,2,64]{0,2,1:T(8,128)S(1)}, bf16[16384,128]{0,1:T(8,128)(2,1)...) while((s32[]{:T(128)}, f32[2,2048]{1,0:T(2,128)S(1)}, ...), condition=%wide.region_5.6_spmd.clone, body=%wide.region_2.5_spmd.clone.sunk | while | flops 1108107264 | bytes 54788264 | solution.py:139
  239.4 8.1 %bitcast_reduce_fusion.2 = (f32[2,2048]{1,0:T(2,128)S(1)}, f32[2,1024,2048]{2,1,0:T(8,128)}) fusion(bf16[1024,2,64]{0,2,1:T(8,128)(2,1)S(1)} %bitcast.134, bf16[2048,2,64]{0,2,1:T(8,128)(2,1)S(1)} %get-tuple-element.339), kind=kOutput, calls=%fused_computation.1.clone.1 | convolution fusion | flops 545255424 | bytes 17580032 | tf_op jit(solution)/shard_map/while/body/eval_jaxpr/qhd,khd->hqk/dot_general | solution.py:124
  254.9 8.5 %fusion.162 = f32[2,2048]{1,0:T(2,128)S(1)} fusion(f32[2,1024,2048]{2,1,0:T(8,128)} %get-tuple-element.309, f32[2,2048]{1,0:T(2,128)S(1)} %get-tuple-element.335), kind=kLoop, calls=%fused_computation.4.clone.1 | loop fusion | flops 12578816 | bytes 16809984 | tf_op jit(solution)/shard_map/while/body/eval_jaxpr/reduce_sum | solution.py:130
  264.6 8.1 %bitcast_reduce_fusion.2 = (f32[2,2048]{1,0:T(2,128)S(1)}, f32[2,1024,2048]{2,1,0:T(8,128)}) fusion(bf16[1024,2,64]{0,2,1:T(8,128)(2,1)S(1)} %bitcast.134, bf16[2048,2,64]{0,2,1:T(8,128)(2,1)S(1)} %get-tuple-element.339), kind=kOutput, calls=%fused_computation.1.clone.1 | convolution fusion | flops 545255424 | bytes 17580032 | tf_op jit(solution)/shard_map/while/body/eval_jaxpr/qhd,khd->hqk/dot_general | solution.py:124
  280.1 8.5 %fusion.162 = f32[2,2048]{1,0:T(2,128)S(1)} fusion(f32[2,1024,2048]{2,1,0:T(8,128)} %get-tuple-element.309, f32[2,2048]{1,0:T(2,128)S(1)} %get-tuple-element.335), kind=kLoop, calls=%fused_computation.4.clone.1 | loop fusion | flops 12578816 | bytes 16809984 | tf_op jit(solution)/shard_map/while/body/eval_jaxpr/reduce_sum | solution.py:130
  289.8 8.1 %bitcast_reduce_fusion.2 = (f32[2,2048]{1,0:T(2,128)S(1)}, f32[2,1024,2048]{2,1,0:T(8,128)}) fusion(bf16[1024,2,64]{0,2,1:T(8,128)(2,1)S(1)} %bitcast.134, bf16[2048,2,64]{0,2,1:T(8,128)(2,1)S(1)} %get-tuple-element.339), kind=kOutput, calls=%fused_computation.1.clone.1 | convolution fusion | flops 545255424 | bytes 17580032 | tf_op jit(solution)/shard_map/while/body/eval_jaxpr/qhd,khd->hqk/dot_general | solution.py:124
  305.3 8.5 %fusion.162 = f32[2,2048]{1,0:T(2,128)S(1)} fusion(f32[2,1024,2048]{2,1,0:T(8,128)} %get-tuple-element.309, f32[2,2048]{1,0:T(2,128)S(1)} %get-tuple-element.335), kind=kLoop, calls=%fused_computation.4.clone.1 | loop fusion | flops 12578816 | bytes 16809984 | tf_op jit(solution)/shard_map/while/body/eval_jaxpr/reduce_sum | solution.py:130
  330.5 8.5 %fusion.162 = f32[2,2048]{1,0:T(2,128)S(1)} fusion(f32[2,1024,2048]{2,1,0:T(8,128)} %get-tuple-element.309, f32[2,2048]{1,0:T(2,128)S(1)} %get-tuple-element.335), kind=kLoop, calls=%fused_computation.4.clone.1 | loop fusion | flops 12578816 | bytes 16809984 | tf_op jit(solution)/shard_map/while/body/eval_jaxpr/reduce_sum | solution.py:130
  340.2 8.1 %bitcast_reduce_fusion.2 = (f32[2,2048]{1,0:T(2,128)S(1)}, f32[2,1024,2048]{2,1,0:T(8,128)}) fusion(bf16[1024,2,64]{0,2,1:T(8,128)(2,1)S(1)} %bitcast.134, bf16[2048,2,64]{0,2,1:T(8,128)(2,1)S(1)} %get-tuple-element.339), kind=kOutput, calls=%fused_computation.1.clone.1 | convolution fusion | flops 545255424 | bytes 17580032 | tf_op jit(solution)/shard_map/while/body/eval_jaxpr/qhd,khd->hqk/dot_general | solution.py:124
  355.8 8.5 %fusion.162 = f32[2,2048]{1,0:T(2,128)S(1)} fusion(f32[2,1024,2048]{2,1,0:T(8,128)} %get-tuple-element.309, f32[2,2048]{1,0:T(2,128)S(1)} %get-tuple-element.335), kind=kLoop, calls=%fused_computation.4.clone.1 | loop fusion | flops 12578816 | bytes 16809984 | tf_op jit(solution)/shard_map/while/body/eval_jaxpr/reduce_sum | solution.py:130
  365.4 8.1 %bitcast_reduce_fusion.2 = (f32[2,2048]{1,0:T(2,128)S(1)}, f32[2,1024,2048]{2,1,0:T(8,128)}) fusion(bf16[1024,2,64]{0,2,1:T(8,128)(2,1)S(1)} %bitcast.134, bf16[2048,2,64]{0,2,1:T(8,128)(2,1)S(1)} %get-tuple-element.339), kind=kOutput, calls=%fused_computation.1.clone.1 | convolution fusion | flops 545255424 | bytes 17580032 | tf_op jit(solution)/shard_map/while/body/eval_jaxpr/qhd,khd->hqk/dot_general | solution.py:124
  381.0 8.5 %fusion.162 = f32[2,2048]{1,0:T(2,128)S(1)} fusion(f32[2,1024,2048]{2,1,0:T(8,128)} %get-tuple-element.309, f32[2,2048]{1,0:T(2,128)S(1)} %get-tuple-element.335), kind=kLoop, calls=%fused_computation.4.clone.1 | loop fusion | flops 12578816 | bytes 16809984 | tf_op jit(solution)/shard_map/while/body/eval_jaxpr/reduce_sum | solution.py:130
  390.6 8.1 %bitcast_reduce_fusion.2 = (f32[2,2048]{1,0:T(2,128)S(1)}, f32[2,1024,2048]{2,1,0:T(8,128)}) fusion(bf16[1024,2,64]{0,2,1:T(8,128)(2,1)S(1)} %bitcast.134, bf16[2048,2,64]{0,2,1:T(8,128)(2,1)S(1)} %get-tuple-element.339), kind=kOutput, calls=%fused_computation.1.clone.1 | convolution fusion | flops 545255424 | bytes 17580032 | tf_op jit(solution)/shard_map/while/body/eval_jaxpr/qhd,khd->hqk/dot_general | solution.py:124
  406.2 8.5 %fusion.162 = f32[2,2048]{1,0:T(2,128)S(1)} fusion(f32[2,1024,2048]{2,1,0:T(8,128)} %get-tuple-element.309, f32[2,2048]{1,0:T(2,128)S(1)} %get-tuple-element.335), kind=kLoop, calls=%fused_computation.4.clone.1 | loop fusion | flops 12578816 | bytes 16809984 | tf_op jit(solution)/shard_map/while/body/eval_jaxpr/reduce_sum | solution.py:130
  431.4 8.5 %fusion.162 = f32[2,2048]{1,0:T(2,128)S(1)} fusion(f32[2,1024,2048]{2,1,0:T(8,128)} %get-tuple-element.309, f32[2,2048]{1,0:T(2,128)S(1)} %get-tuple-element.335), kind=kLoop, calls=%fused_computation.4.clone.1 | loop fusion | flops 12578816 | bytes 16809984 | tf_op jit(solution)/shard_map/while/body/eval_jaxpr/reduce_sum | solution.py:130
  441.0 8.1 %bitcast_reduce_fusion.2 = (f32[2,2048]{1,0:T(2,128)S(1)}, f32[2,1024,2048]{2,1,0:T(8,128)}) fusion(bf16[1024,2,64]{0,2,1:T(8,128)(2,1)S(1)} %bitcast.134, bf16[2048,2,64]{0,2,1:T(8,128)(2,1)S(1)} %get-tuple-element.339), kind=kOutput, calls=%fused_computation.1.clone.1 | convolution fusion | flops 545255424 | bytes 17580032 | tf_op jit(solution)/shard_map/while/body/eval_jaxpr/qhd,khd->hqk/dot_general | solution.py:124
  456.6 8.5 %fusion.162 = f32[2,2048]{1,0:T(2,128)S(1)} fusion(f32[2,1024,2048]{2,1,0:T(8,128)} %get-tuple-element.309, f32[2,2048]{1,0:T(2,128)S(1)} %get-tuple-element.335), kind=kLoop, calls=%fused_computation.4.clone.1 | loop fusion | flops 12578816 | bytes 16809984 | tf_op jit(solution)/shard_map/while/body/eval_jaxpr/reduce_sum | solution.py:130
  466.3 8.1 %bitcast_reduce_fusion.2 = (f32[2,2048]{1,0:T(2,128)S(1)}, f32[2,1024,2048]{2,1,0:T(8,128)}) fusion(bf16[1024,2,64]{0,2,1:T(8,128)(2,1)S(1)} %bitcast.134, bf16[2048,2,64]{0,2,1:T(8,128)(2,1)S(1)} %get-tuple-element.339), kind=kOutput, calls=%fused_computation.1.clone.1 | convolution fusion | flops 545255424 | bytes 17580032 | tf_op jit(solution)/shard_map/while/body/eval_jaxpr/qhd,khd->hqk/dot_general | solution.py:124
  481.8 8.5 %fusion.162 = f32[2,2048]{1,0:T(2,128)S(1)} fusion(f32[2,1024,2048]{2,1,0:T(8,128)} %get-tuple-element.309, f32[2,2048]{1,0:T(2,128)S(1)} %get-tuple-element.335), kind=kLoop, calls=%fused_computation.4.clone.1 | loop fusion | flops 12578816 | bytes 16809984 | tf_op jit(solution)/shard_map/while/body/eval_jaxpr/reduce_sum | solution.py:130
  507.0 8.5 %fusion.162 = f32[2,2048]{1,0:T(2,128)S(1)} fusion(f32[2,1024,2048]{2,1,0:T(8,128)} %get-tuple-element.309, f32[2,2048]{1,0:T(2,128)S(1)} %get-tuple-element.335), kind=kLoop, calls=%fused_computation.4.clone.1 | loop fusion | flops 12578816 | bytes 16809984 | tf_op jit(solution)/shard_map/while/body/eval_jaxpr/reduce_sum | solution.py:130
  532.2 8.5 %fusion.162 = f32[2,2048]{1,0:T(2,128)S(1)} fusion(f32[2,1024,2048]{2,1,0:T(8,128)} %get-tuple-element.309, f32[2,2048]{1,0:T(2,128)S(1)} %get-tuple-element.335), kind=kLoop, calls=%fused_computation.4.clone.1 | loop fusion | flops 12578816 | bytes 16809984 | tf_op jit(solution)/shard_map/while/body/eval_jaxpr/reduce_sum | solution.py:130
  541.9 8.1 %bitcast_reduce_fusion.2 = (f32[2,2048]{1,0:T(2,128)S(1)}, f32[2,1024,2048]{2,1,0:T(8,128)}) fusion(bf16[1024,2,64]{0,2,1:T(8,128)(2,1)S(1)} %bitcast.134, bf16[2048,2,64]{0,2,1:T(8,128)(2,1)S(1)} %get-tuple-element.339), kind=kOutput, calls=%fused_computation.1.clone.1 | convolution fusion | flops 545255424 | bytes 17580032 | tf_op jit(solution)/shard_map/while/body/eval_jaxpr/qhd,khd->hqk/dot_general | solution.py:124
  557.4 8.5 %fusion.162 = f32[2,2048]{1,0:T(2,128)S(1)} fusion(f32[2,1024,2048]{2,1,0:T(8,128)} %get-tuple-element.309, f32[2,2048]{1,0:T(2,128)S(1)} %get-tuple-element.335), kind=kLoop, calls=%fused_computation.4.clone.1 | loop fusion | flops 12578816 | bytes 16809984 | tf_op jit(solution)/shard_map/while/body/eval_jaxpr/reduce_sum | solution.py:130
  567.1 8.1 %bitcast_reduce_fusion.2 = (f32[2,2048]{1,0:T(2,128)S(1)}, f32[2,1024,2048]{2,1,0:T(8,128)}) fusion(bf16[1024,2,64]{0,2,1:T(8,128)(2,1)S(1)} %bitcast.134, bf16[2048,2,64]{0,2,1:T(8,128)(2,1)S(1)} %get-tuple-element.339), kind=kOutput, calls=%fused_computation.1.clone.1 | convolution fusion | flops 545255424 | bytes 17580032 | tf_op jit(solution)/shard_map/while/body/eval_jaxpr/qhd,khd->hqk/dot_general | solution.py:124
  582.7 8.5 %fusion.162 = f32[2,2048]{1,0:T(2,128)S(1)} fusion(f32[2,1024,2048]{2,1,0:T(8,128)} %get-tuple-element.309, f32[2,2048]{1,0:T(2,128)S(1)} %get-tuple-element.335), kind=kLoop, calls=%fused_computation.4.clone.1 | loop fusion | flops 12578816 | bytes 16809984 | tf_op jit(solution)/shard_map/while/body/eval_jaxpr/reduce_sum | solution.py:130
  607.9 8.5 %fusion.162 = f32[2,2048]{1,0:T(2,128)S(1)} fusion(f32[2,1024,2048]{2,1,0:T(8,128)} %get-tuple-element.309, f32[2,2048]{1,0:T(2,128)S(1)} %get-tuple-element.335), kind=kLoop, calls=%fused_computation.4.clone.1 | loop fusion | flops 12578816 | bytes 16809984 | tf_op jit(solution)/shard_map/while/body/eval_jaxpr/reduce_sum | solution.py:130
  633.1 8.5 %fusion.162 = f32[2,2048]{1,0:T(2,128)S(1)} fusion(f32[2,1024,2048]{2,1,0:T(8,128)} %get-tuple-element.309, f32[2,2048]{1,0:T(2,128)S(1)} %get-tuple-element.335), kind=kLoop, calls=%fused_computation.4.clone.1 | loop fusion | flops 12578816 | bytes 16809984 | tf_op jit(solution)/shard_map/while/body/eval_jaxpr/reduce_sum | solution.py:130
  642.7 15.0 %all_to_all.11 = bf16[16,128,128]{2,1,0:T(8,128)(2,1)S(1)} all-to-all(bf16[16,128,128]{2,1,0:T(8,128)(2,1)S(1)} %bitcast.156), channel_id=1, replica_groups=mesh['aa'=8,'ba'=16] {'ba'}, dimensions={0} | all-to-all | bytes 1048576 | tf_op jit(solution)/shard_map/all_to_all | solution.py:59
  (209 shorter events, 274.3 us)
Async XLA Ops:
  6.5 90.4 %copy-start = (bf16[128,2048]{1,0:T(8,128)(2,1)S(1)}, bf16[128,2048]{1,0:T(8,128)(2,1)}, u32[]{:S(2)}) copy-start(bf16[128,2048]{1,0:T(8,128)(2,1)} %param.23) | copy-start | bytes 1572868
  6.5 225.9 %all-gather.2.cloned.1.call-start = ((), (), s32[]{:S(2)}) async-start(), calls=%async_computation.2 | async-start | bytes 9437184 | tf_op jit(solution)/shard_map/all_gather | solution.py:30
  6.5 9.8 %collective-permute-start = (bf16[1,4,128,256]{3,2,1,0:T(8,128)(2,1)}, bf16[1,4,128,256]{3,2,1,0:T(8,128)(2,1)S(1)}, u32[]{:S(2)}, u32[]{:S(2)}) collective-permute-start(bf16[1,4,128,256]{3,2,1,0:T(8,128)(2,1)} %param.16), channel_id=1, source_target_pairs={{0,16},{16,32},{32,48},{48,64},{64,80},{80,96},{96,112},{1,17},{17... | collective-permute-start | bytes 786440 | tf_op jit(solution)/shard_map/ppermute | solution.py:19
  11.1 9.3 %collective-permute-start.1 = (bf16[1,4,128,256]{3,2,1,0:T(8,128)(2,1)}, bf16[1,4,128,256]{3,2,1,0:T(8,128)(2,1)S(1)}, u32[]{:S(2)}, u32[]{:S(2)}) collective-permute-start(bf16[1,4,128,256]{3,2,1,0:T(8,128)(2,1)} %param.16), channel_id=1, source_target_pairs={{16,0},{32,16},{48,32},{64,48},{80,64},{96,80},{112,96},{17,1},{33... | collective-permute-start | bytes 786440 | tf_op jit(solution)/shard_map/ppermute | solution.py:21
  20.4 8.9 %collective-permute-start.2 = (bf16[3,1,128,256]{3,2,1,0:T(8,128)(2,1)S(1)}, bf16[3,1,128,256]{3,2,1,0:T(8,128)(2,1)S(1)}, u32[]{:S(2)}, u32[]{:S(2)}) collective-permute-start(bf16[3,1,128,256]{3,2,1,0:T(8,128)(2,1)S(1)} %get-tuple-element.247), channel_id=1, source_target_pairs={{0,1},{1,2},{2,3},{3,4},{4,5},{5,6},{6,7},{7,8},{8,9},{9,10},{10,1... | collective-permute-start | bytes 589832 | tf_op jit(solution)/shard_map/ppermute | solution.py:19
  25.2 7.0 %collective-permute-start.3 = (bf16[3,1,128,256]{3,2,1,0:T(8,128)(2,1)S(1)}, bf16[3,1,128,256]{3,2,1,0:T(8,128)(2,1)S(1)}, u32[]{:S(2)}, u32[]{:S(2)}) collective-permute-start(bf16[3,1,128,256]{3,2,1,0:T(8,128)(2,1)S(1)} %get-tuple-element.246), channel_id=1, source_target_pairs={{1,0},{2,1},{3,2},{4,3},{5,4},{6,5},{7,6},{8,7},{9,8},{10,9},{11,1... | collective-permute-start | bytes 589832 | tf_op jit(solution)/shard_map/ppermute | solution.py:21
  32.8 1.0 copy-start.11
  37.8 22.0 %copy-start.3 = (bf16[3,3,3,256,256]{4,3,2,1,0:T(8,128)(2,1)S(1)}, bf16[3,3,3,256,256]{4,3,2,1,0:T(8,128)(2,1)}, u32[]{:S(2)}) copy-start(bf16[3,3,3,256,256]{4,3,2,1,0:T(8,128)(2,1)} %param.19) | copy-start | bytes 10616836
  41.0 6.7 %collective-permute-start.4 = (bf16[1,4,128,256]{3,2,1,0:T(8,128)(2,1)S(1)}, bf16[1,4,128,256]{3,2,1,0:T(8,128)(2,1)S(1)}, u32[]{:S(2)}, u32[]{:S(2)}) collective-permute-start(bf16[1,4,128,256]{3,2,1,0:T(8,128)(2,1)S(1)} %fusion.61), channel_id=1, source_target_pairs={{0,16},{16,32},{32,48},{48,64},{64,80},{80,96},{96,112},{1,17},{17... | collective-permute-start | bytes 786440 | tf_op jit(solution)/shard_map/ppermute | solution.py:19
  44.4 7.1 %collective-permute-start.5 = (bf16[1,4,128,256]{3,2,1,0:T(8,128)(2,1)S(1)}, bf16[1,4,128,256]{3,2,1,0:T(8,128)(2,1)S(1)}, u32[]{:S(2)}, u32[]{:S(2)}) collective-permute-start(bf16[1,4,128,256]{3,2,1,0:T(8,128)(2,1)S(1)} %fusion.61), channel_id=1, source_target_pairs={{16,0},{32,16},{48,32},{64,48},{80,64},{96,80},{112,96},{17,1},{33... | collective-permute-start | bytes 786440 | tf_op jit(solution)/shard_map/ppermute | solution.py:21
  52.3 9.9 %collective-permute-start.6 = (bf16[3,1,128,256]{3,2,1,0:T(8,128)(2,1)}, bf16[3,1,128,256]{3,2,1,0:T(8,128)(2,1)}, u32[]{:S(2)}, u32[]{:S(2)}) collective-permute-start(bf16[3,1,128,256]{3,2,1,0:T(8,128)(2,1)} %get-tuple-element.245), channel_id=1, source_target_pairs={{0,1},{1,2},{2,3},{3,4},{4,5},{5,6},{6,7},{7,8},{8,9},{9,10},{10,1... | collective-permute-start | bytes 589832 | tf_op jit(solution)/shard_map/ppermute | solution.py:19
  57.7 7.2 %collective-permute-start.7 = (bf16[3,1,128,256]{3,2,1,0:T(8,128)(2,1)}, bf16[3,1,128,256]{3,2,1,0:T(8,128)(2,1)S(1)}, u32[]{:S(2)}, u32[]{:S(2)}) collective-permute-start(bf16[3,1,128,256]{3,2,1,0:T(8,128)(2,1)} %get-tuple-element.244), channel_id=1, source_target_pairs={{1,0},{2,1},{3,2},{4,3},{5,4},{6,5},{7,6},{8,7},{9,8},{10,9},{11,1... | collective-permute-start | bytes 589832 | tf_op jit(solution)/shard_map/ppermute | solution.py:21
  67.3 1.1 copy-start.10
  68.4 1.0 copy-start.9
  69.8 1.0 copy-start.8
  70.1 1.1 copy-start.7
  71.2 1.0 copy-start.12
  71.2 1.1 copy-start.22
  71.6 1.1 copy-start.6
  72.6 1.0 copy-start.5
  73.6 1.0 copy-start.4
  74.0 1.0 copy-start.15
  76.1 2.7 copy-start.16
  78.3 18.6 %copy-start.13 = (f32[2048]{0:T(1024)S(1)}, f32[2048]{0:T(1024)}, u32[]{:S(2)}) copy-start(f32[2048]{0:T(1024)} %param.24) | copy-start | bytes 24580
  104.0 8.2 %copy-start.17 = (bf16[2048,128]{1,0:T(8,128)(2,1)S(1)}, bf16[2048,128]{1,0:T(8,128)(2,1)}, u32[]{:S(2)}) copy-start(bf16[2048,128]{1,0:T(8,128)(2,1)} %param.28) | copy-start | bytes 1572868
  104.0 8.2 %copy-start.18 = (bf16[2048,128]{1,0:T(8,128)(2,1)S(1)}, bf16[2048,128]{1,0:T(8,128)(2,1)}, u32[]{:S(2)}) copy-start(bf16[2048,128]{1,0:T(8,128)(2,1)} %param.27) | copy-start | bytes 1572868
  104.0 8.2 %copy-start.19 = (bf16[2048,128]{1,0:T(8,128)(2,1)S(1)}, bf16[2048,128]{1,0:T(8,128)(2,1)}, u32[]{:S(2)}) copy-start(bf16[2048,128]{1,0:T(8,128)(2,1)} %param.26) | copy-start | bytes 1572868
  104.0 8.2 %copy-start.20 = (f32[2048]{0:T(1024)S(1)}, f32[2048]{0:T(1024)}, u32[]{:S(2)}) copy-start(f32[2048]{0:T(1024)} %param.25) | copy-start | bytes 24580
  121.2 1.5 copy-start.2
  122.7 115.6 %slice-start = ((bf16[2048,384]{0,1:T(8,128)(2,1)}), bf16[2048,128]{0,1:T(8,128)(2,1)S(1)}, s32[]{:S(2)}) async-start(bf16[2048,384]{0,1:T(8,128)(2,1)} %copy-done.2), calls=%async_computation.3 | async-start | bytes 1048576 | tf_op jit(solution)/shard_map/slice | solution.py:172
  641.6 0.8 copy-start.14
  641.7 16.8 %copy-start.1 = (bf16[128,2048]{1,0:T(8,128)(2,1)S(1)}, bf16[128,2048]{1,0:T(8,128)(2,1)}, u32[]{:S(2)}) copy-start(bf16[128,2048]{1,0:T(8,128)(2,1)} %param.23) | copy-start | bytes 1572868
  (1 other events, 0.7 us)
Sparse Core Ops, SparseCore 0:
  122.5 109.8 all-gather.1
where the time goes:
time: 667 us; the launch traced here: 665 us
  matrix products  274 us (41%)
  other arithmetic  155 us (23%)
  waiting for transfers between devices  128 us (19%)
  local copies, waits for them, and re-layouts  36.9 us (6%)
  blocking collectives  31.8 us (5%)
  starting transfers between devices  24.7 us (4%)
  between operations  14.1 us (2%)
    reduce_sum x16, other arithmetic, one_step(): denom = denom * fade + probs.sum(-1)  136 us
    dot_general x16, matrix products, one_step(): jnp.einsum('qhd,khd->hqk', query_heads, key_block, preferred_element_type...  130 us
    dot_general x16, matrix products, one_step(): jnp.einsum('hqk,khd->qhd', probs.astype(jnp.bfloat16), value_block, prefe...  118 us
    all_gather x1, waiting for transfers between devices, side_by_side(): lax.all_gather(both, axis, axis=dim, tiled=True)  110 us
    ppermute x4, starting transfers between devices, with_halo(): lax.ppermute(tail, axis, [(i, (i + 1) % count) for i in range(ends)])  18.1 us
    dynamic_slice x16, local copies, waits for them, and re-layouts, one_step(): lax.dynamic_slice_in_dim(value_rows, index * block, block, 0)  17.1 us
    all_to_all x1, blocking collectives, copy_for_each(): return lax.all_to_all(copies, axis, split_axis=0, concat_axis=0, tiled=True)  16.8 us
    all_to_all x1, blocking collectives, sent_and_summed(): parts = lax.all_to_all(cut_along(x, dim, peers), axis, 0, 0, tiled=True)  15 us
  transfers between devices with their start and end apart: 9, of which 7 were waited for; matrix products, arithmetic and copies ran while one was open for 1% of the time, Pallas kernels for 0%

commit v1 on v0

v1 whole, which is shorter than its diff:
```python
import functools
import math

import jax
import jax.numpy as jnp
from jax import lax
from jax.experimental import pallas as pl
from jax.experimental.pallas import tpu as pltpu
from jax.sharding import PartitionSpec as P

HEAD_DIM = 64
BF = jnp.bfloat16
F32 = jnp.float32
DEPTH = 144
TILE = 128
SAMPLE = 2
MIB = 2**20
TN = (((0,), (0,)), ((), ()))
HI = lax.Precision.HIGHEST


def gelu(x):
    return 0.5 * x * (1.0 + lax.erf(x * (1.0 / math.sqrt(2.0))))


def neighbours(block, row_axis):
    na, nb = lax.axis_size("aa"), lax.axis_size("ba")

    def shift(x, da, db):
        pairs = []
        for a in range(na):
            for b in range(nb):
                if 0 <= a + da < na and 0 <= b + db < nb:
                    pairs.append((a * nb + b, (a + da) * nb + b + db))
        return lax.ppermute(x, ("aa", "ba"), pairs)

    top, bottom = block[:1], block[-1:]
    before = shift(block, 1, 0)
    after = shift(block, -1, 0)
    ups = [shift(bottom, da, 1) for da in (1, 0, -1)]
    downs = [shift(top, da, -1) for da in (1, 0, -1)]
    return (before, block, after, *ups, *downs)


def conv_taps(refs, w_ref, pad_ref, acc_ref):
    step = pl.program_id(0)
    rows, width, chans = refs[1].shape

    @pl.when(step == 0)
    def _():
        for t in range(3):
            pad_ref[t, 0:width] = refs[3 + t][0]
            for r in range(rows):
                pad_ref[t, (r + 1) * width : (r + 2) * width] = refs[t][r]
            pad_ref[t, (rows + 1) * width : (rows + 2) * width] = refs[6 + t][0]

    for w in range(3):
        total = jnp.dot(pad_ref[step, 0 : rows * width], w_ref[0, 0, w], preferred_element_type=F32)
        for r in (1, 2):
            total += jnp.dot(
                pad_ref[step, r * width : (r + rows) * width],
                w_ref[0, r, w],
                preferred_element_type=F32,
            )

        @pl.when(step == 0)
        def _():
            acc_ref[w] = total

        @pl.when(step > 0)
        def _():
            acc_ref[w] += total


def conv_sum(acc_ref, bias_ref, width):
    count = acc_ref.shape[1]
    at = lax.broadcasted_iota(jnp.int32, (count, 1), 0) % width
    left = jnp.where(at == 0, 0.0, pltpu.roll(acc_ref[0], 1, 0))
    right = jnp.where(at == width - 1, 0.0, pltpu.roll(acc_ref[2], count - 1, 0))
    return left + acc_ref[1] + right + bias_ref[...]


def first_kernel(*refs):
    halo, (w_ref, bias_ref, out_ref, pad_ref, acc_ref) = refs[:9], refs[9:]
    conv_taps(halo, w_ref, pad_ref, acc_ref)

    @pl.when(pl.program_id(0) == 2)
    def _():
        rows, width, chans = out_ref.shape
        out_ref[...] = gelu(conv_sum(acc_ref, bias_ref, width)).astype(BF).reshape(rows, width, chans)


def second_kernel(*refs):
    halo, (w_ref, bias_ref, pw_ref, pb_ref, out_ref, pad_ref, acc_ref) = refs[:9], refs[9:]
    conv_taps(halo, w_ref, pad_ref, acc_ref)

    @pl.when(pl.program_id(0) == 2)
    def _():
        rows, width, chans = halo[1].shape
        half = width // 2
        first = halo[1][...].reshape(rows * width, chans).astype(F32)
        second = (first + gelu(conv_sum(acc_ref, bias_ref, width))).astype(BF)
        r = lax.broadcasted_iota(jnp.int32, (width, width), 0)
        c = lax.broadcasted_iota(jnp.int32, (width, width), 1)
        picks = (c == jnp.where(r < half, 2 * r, 2 * r - (width - 1))).astype(BF)
        for e in range(rows // 2):
            total = pb_ref[...] + jnp.zeros((half, pb_ref.shape[1]), F32)
            for a in range(2):
                at = (2 * e + a) * width
                sorted_row = jnp.dot(
                    picks, second[at : at + width], preferred_element_type=F32
                ).astype(BF)
                for k in range(2):
                    total += jnp.dot(
                        sorted_row[k * half : (k + 1) * half],
                        pw_ref[a, k],
                        preferred_element_type=F32,
                    )
            out_ref[e * half : (e + 1) * half] = total.astype(BF)


def conv_call(kernel, halo, weight, extras, out_shape):
    rows, width, chans = halo[1].shape
    whole = [pl.BlockSpec(memory_space=pltpu.VMEM)]
    return pl.pallas_call(
        kernel,
        grid=(3,),
        in_specs=whole * 9
        + [pl.BlockSpec((1, 3, 3, chans, chans), lambda i: (i, 0, 0, 0, 0))]
        + whole * len(extras),
        out_specs=pl.BlockSpec(memory_space=pltpu.VMEM),
        out_shape=jax.ShapeDtypeStruct(out_shape, BF),
        scratch_shapes=[
            pltpu.VMEM((3, (rows + 2) * width, chans), BF),
            pltpu.VMEM((3, rows * width, chans), F32),
        ],
        compiler_params=pltpu.CompilerParams(vmem_limit_bytes=32 * MIB),
        cost_estimate=pl.CostEstimate(
            flops=2 * 27 * rows * width * chans * chans,
            bytes_accessed=2 * 27 * chans * chans,
            transcendentals=0,
        ),
    )(*halo, weight, *extras)


def side(tiles):
    return jnp.concatenate(tiles, axis=1)


def attend_kernel(n_blocks, start, finish, heads, *refs):
    q_ref, *rest = refs
    blocks, rest = rest[:n_blocks], rest[n_blocks:]
    if not start:
        (m_in, o_in, *rest) = rest
    if finish:
        n_all = len(rest) - 3
        everything, (out_ref, held, sem) = rest[:n_all], rest[n_all:]
    else:
        m_out, out_ref = rest
    query = side([q_ref[h] for h in range(heads)])

    def scores(tiles):
        return lax.dot_general(tiles, query, TN, preferred_element_type=F32)

    if start:
        sample = side([blocks[0][i] for i in range(SAMPLE)])
        shift = scores(sample).max(0, keepdims=True)
        total = jnp.zeros((DEPTH, heads * TILE), F32)
    else:
        shift = m_in[...]
        total = side([o_in[h] for h in range(heads)])
    for block in blocks:
        keys = side([block[i] for i in range(block.shape[0])])
        probs = jnp.exp2(scores(keys) - shift).astype(BF)
        total = total + jnp.dot(keys, probs, preferred_element_type=F32)
    if not finish:
        m_out[...] = shift
        for h in range(heads):
            out_ref[h] = total[:, h * TILE : (h + 1) * TILE]
        return

    def store(sums):
        scaled = (sums / sums[TILE + 1 : TILE + 2]).astype(BF)
        for h in range(heads):
            out_ref[h] = scaled[:, h * TILE : (h + 1) * TILE]

    store(total)
    largest = jnp.where(total[TILE + 1 : TILE + 2] < 2.0**100, 0.0, 1.0).max()

    @pl.when(largest > 0.5)
    def _():
        state = (
            jnp.full((1, heads * TILE), -1e38, F32),
            jnp.zeros((DEPTH, heads * TILE), F32),
        )
        for source in everything:
            copy = pltpu.make_async_copy(source, held, sem)
            copy.start()
            copy.wait()

            def one_tile(i, state):
                best, sums = state
                keys = held[i]
                s = scores(keys)
                peak = jnp.maximum(best, s.max(0, keepdims=True))
                probs = jnp.exp2(s - peak).astype(BF)
                sums = sums * jnp.exp2(best - peak) + jnp.dot(
                    keys, probs, preferred_element_type=F32
                )
                return peak, sums

            state = lax.fori_loop(0, held.shape[0], one_tile, state)
        store(state[1])


def attend_call(queries, blocks, state, everything, heads):
    n_heads = queries.shape[0]
    start, finish = state is None, everything is not None
    per_q = pl.BlockSpec((heads, DEPTH, TILE), lambda i: (i, 0, 0))
    per_m = pl.BlockSpec((1, heads * TILE), lambda i: (0, i))
    whole = pl.BlockSpec(memory_space=pltpu.VMEM)
    args, specs = [queries, *blocks], [per_q] + [whole] * len(blocks)
    if not start:
        args += state
        specs += [per_m, per_q]
    scratch = []
    if finish:
        args += everything
        specs += [pl.BlockSpec(memory_space=pl.ANY)] * len(everything)
        out_specs = per_q
        out_shape = jax.ShapeDtypeStruct(queries.shape, BF)
        scratch = [pltpu.VMEM(blocks[0].shape, BF), pltpu.SemaphoreType.DMA(())]
    else:
        out_specs = [per_m, per_q]
        out_shape = [
            jax.ShapeDtypeStruct((1, n_heads * TILE), F32),
            jax.ShapeDtypeStruct(queries.shape, F32),
        ]
    pairs = n_heads * TILE * sum(b.shape[0] for b in blocks) * TILE
    return pl.pallas_call(
        functools.partial(attend_kernel, len(blocks), start, finish, heads),
        grid=(n_heads // heads,),
        in_specs=specs,
        out_specs=out_specs,
        out_shape=out_shape,
        scratch_shapes=scratch,
        compiler_params=pltpu.CompilerParams(vmem_limit_bytes=58 * MIB),
        cost_estimate=pl.CostEstimate(
            flops=pairs * 1024, bytes_accessed=4 * MIB, transcendentals=pairs
        ),
    )(*args)


def projections(embed_weight, embed_bias, norm_gain, w_query, w_key, w_value, w_velocity):
    width = w_query.shape[1]
    heads = width // HEAD_DIM
    latent, features = embed_weight.shape
    embed = jnp.concatenate(
        [
            embed_weight.astype(F32),
            embed_bias[None],
            jnp.zeros((DEPTH - latent - 1, features), F32),
        ],
        axis=0,
    )
    embed = embed - embed.mean(1, keepdims=True)
    gram = lax.dot_general(embed, embed, (((1,), (1,)), ((), ())), precision=HI) / features
    gained = embed * norm_gain
    high = gained.astype(BF)
    low = (gained - high.astype(F32)).astype(BF)
    joined = jnp.dot(
        jnp.concatenate([high, low], axis=0),
        jnp.concatenate([w_query, w_key, w_value], axis=1),
        preferred_element_type=F32,
    )
    joined = (joined[:DEPTH] + joined[DEPTH:]).reshape(DEPTH, 3, heads, HEAD_DIM)
    scale = HEAD_DIM ** (-0.5) * math.log2(math.e)
    forms = jnp.einsum("ehf,dhf->hed", joined[:, 1], joined[:, 0] * scale, precision=HI)
    outs = jnp.einsum(
        "ehf,hfc->hec",
        joined[:, 2],
        w_velocity.astype(F32).reshape(heads, HEAD_DIM, -1),
        precision=HI,
    )
    return gram, jnp.concatenate([outs, forms], axis=-1).astype(BF)


def copy_for_each(x, axis):
    copies = jnp.broadcast_to(x, (lax.axis_size(axis), *x.shape))
    return lax.all_to_all(copies, axis, split_axis=0, concat_axis=0, tiled=True)


def on_device(
    feats,
    conv_one,
    bias_one,
    conv_two,
    bias_two,
    patch_weight,
    patch_bias,
    embed_weight,
    embed_bias,
    norm_gain,
    w_query,
    w_key,
    w_value,
    w_velocity,
):
    rows, width, chans = feats.shape[1:]
    gram, maps = projections(
        embed_weight, embed_bias, norm_gain, w_query, w_key, w_value, w_velocity
    )
    maps = lax.all_gather(maps, "ba", axis=0, tiled=True)
    n_heads = maps.shape[0]

    halo = neighbours(feats[0], 0)
    first = conv_call(first_kernel, halo, conv_one, [bias_one[None]], (rows, width, chans))
    halo = neighbours(first, 0)
    tokens = rows * width // 4
    latents = conv_call(
        second_kernel,
        halo,
        conv_two,
        [bias_two[None], patch_weight, patch_bias[None]],
        (tokens, patch_bias.shape[0]),
    )

    ones = jnp.ones((1, tokens), F32)
    spare = jnp.zeros((DEPTH - TILE - 2, tokens), F32)
    columns = jnp.concatenate([latents.astype(F32).T, ones, 0 * ones, spare], axis=0)
    spread = (columns * jnp.dot(gram, columns, precision=HI)).sum(0, keepdims=True)
    rstd = lax.rsqrt(jnp.maximum(spread, 0.0) + 1e-05)
    own = jnp.concatenate([(columns * rstd)[: TILE + 1], ones, spare], axis=0).astype(BF)

    block = copy_for_each(own, "ba")
    count = lax.axis_size("aa")
    inner = count // 2
    blocks = [block]
    for dx, dz in ((0, 1), (0, 3), (1, 0), (0, 2), (1, 1), (1, 3), (1, 2)):
        pairs = [
            (x * inner + z, (x + dx) % 2 * inner + (z + dz) % inner)
            for x in range(2)
            for z in range(inner)
        ]
        blocks.append(lax.ppermute(block, "aa", pairs))

    forms = maps[:, :, TILE:].reshape(n_heads * DEPTH, DEPTH)
    queries = jnp.dot(forms, columns.astype(BF), preferred_element_type=F32) * rstd
    queries = queries.astype(BF).reshape(n_heads, DEPTH, tokens)

    state = attend_call(queries, blocks[:1], None, None, 8)
    state = attend_call(queries, blocks[1:2], state, None, 8)
    state = attend_call(queries, blocks[2:4], state, None, 8)
    attended = attend_call(queries, blocks[4:], state, blocks, 8)
    outs = maps[:, :, :TILE].reshape(n_heads * DEPTH, TILE)
    return lax.dot_general(
        attended.reshape(n_heads * DEPTH, tokens), outs, TN, preferred_element_type=F32
    )


def solution(mesh):
    return jax.shard_map(
        on_device,
        mesh=mesh,
        in_specs=(
            P("aa", "ba", None, None),
            P(),
            P(),
            P(),
            P(),
            P(),
            P(),
            P(),
            P(),
            P(),
            P(None, "ba"),
            P(None, "ba"),
            P(None, "ba"),
            P("ba", None),
        ),
        out_specs=P(("aa", "ba"), None),
        check_vma=False,
    )
```

time: 667 us -> 236 us (0.35)
  matrix products: 274 us -> 7.52 us
  other arithmetic: 155 us -> 2.61 us
  waiting for transfers between devices: 128 us -> 13.3 us
  Pallas kernels: 0 us -> 81.3 us
  starting transfers between devices: 24.7 us -> 88.4 us
  local copies, waits for them, and re-layouts: 36.9 us -> 7.5 us
  blocking collectives: 31.8 us -> 17 us
    dot_general x54 -> x7, matrix products: 274 us -> 7.52 us  [the longest x1 2.43 us: on_device(): lax.dot_general(attended.reshape(n_heads * DEPTH, tokens), outs, TN, pref...]
    reduce_sum x18 -> x1, other arithmetic: 145 us -> 0.23 us  [projections(): embed = embed - embed.mean(1, keepdims=True)]
    all_gather x1, waiting for transfers between devices: 110 us -> 0.01 us  [on_device(): maps = lax.all_gather(maps, 'ba', axis=0, tiled=True)]
    pallas_call x0 -> x6, Pallas kernels: none -> 81.3 us  [the longest x4 70.7 us: attend_call(): pl.pallas_call(functools.partial(attend_kernel, len(blocks), start, finis...]
    ppermute x8 -> x23, starting transfers between devices: 24.7 us -> 88.4 us  [the longest x16 51.7 us: shift(): return lax.ppermute(x, ('aa', 'ba'), pairs)]
    dynamic_slice x16 -> x0, local copies, waits for them, and re-layouts: 17.1 us -> none  [one_step(): lax.dynamic_slice_in_dim(value_rows, index * block, block, 0)]
    all_to_all x1 -> x0, blocking collectives: 15 us -> none  [sent_and_summed(): parts = lax.all_to_all(cut_along(x, dim, peers), axis, 0, 0, tiled=True)]
    slice x8 -> x4, local copies, waits for them, and re-layouts: 11.5 us -> 1.68 us  [the longest x2 1.66 us: on_device(): forms = maps[:, :, TILE:].reshape(n_heads * DEPTH, DEPTH)]
  transfers between devices with their start and end apart: 9 -> 24, of which waited for: 7 -> 4; matrix products, arithmetic and copies ran while one was open for 1% -> 2% of each run, Pallas kernels for 0% -> 21%
where the time goes in v1:
time: 236 us; the launch traced here: 232 us
  starting transfers between devices  88.4 us (37%)
  Pallas kernels  81.3 us (34%)
  blocking collectives  17 us (7%)
  between operations  14 us (6%)
  waiting for transfers between devices  13.3 us (6%)
  matrix products  7.52 us (3%)
  local copies, waits for them, and re-layouts  7.5 us (3%)
  other arithmetic  2.61 us (1%)
    pallas_call x4, Pallas kernels, attend_call(): pl.pallas_call(functools.partial(attend_kernel, len(blocks), start, finis...  70.7 us
    ppermute x16, starting transfers between devices, shift(): return lax.ppermute(x, ('aa', 'ba'), pairs)  51.7 us
    ppermute x7, starting transfers between devices, on_device(): blocks.append(lax.ppermute(block, 'aa', pairs))  36.7 us
    all_to_all x1, blocking collectives, copy_for_each(): return lax.all_to_all(copies, axis, split_axis=0, concat_axis=0, tiled=True)  17 us
    ppermute x16, waiting for transfers between devices, shift(): return lax.ppermute(x, ('aa', 'ba'), pairs)  13.3 us
    pallas_call x2, Pallas kernels, conv_call(): pl.pallas_call(kernel, grid=(3,), in_specs=whole * 9 + [pl.BlockSpec((1,...  10.6 us
    unnamed x42, local copies, waits for them, and re-layouts  5.08 us
  transfers between devices with their start and end apart: 24, of which 4 were waited for; matrix products, arithmetic and copies ran while one was open for 2% of the time, Pallas kernels for 21%

profile of v1, /device:TPU:1, one launch (start us, length us, event | category | flops | bytes accessed | tf_op | source)
XLA Modules:
  0.0 231.7 jit_solution(4257035193170591099)
XLA Ops:
  12.0 4.4 %collective-permute-start = (bf16[4,128,256]{2,1,0:T(8,128)(2,1)S(1)}, bf16[4,128,256]{2,1,0:T(8,128)(2,1)S(1)}, u32[]{:S(2)}, u32[]{:S(2)}) collective-permute-start(bf16[4,128,256]{2,1,0:T(8,128)(2,1)S(1)} %bitcast.34), channel_id=1, source_target_pairs={{0,16},{1,17},{2,18},{3,19},{4,20},{5,21},{6,22},{7,23},{8,24},{9,... | collective-permute-start | bytes 786440 | tf_op jit(solution)/shard_map/ppermute | solution.py:35
  17.7 6.1 %collective-permute-start.2 = (bf16[1,128,256]{2,1,0:T(8,128)(2,1)S(1)}, bf16[1,128,256]{2,1,0:T(8,128)(2,1)S(1)}, u32[]{:S(2)}, u32[]{:S(2)}) collective-permute-start(bf16[1,128,256]{2,1,0:T(8,128)(2,1)S(1)} %get-tuple-element.22), channel_id=1, source_target_pairs={{0,17},{1,18},{2,19},{3,20},{4,21},{5,22},{6,23},{7,24},{8,25},{9,... | collective-permute-start | bytes 196616 | tf_op jit(solution)/shard_map/ppermute | solution.py:35
  23.9 1.9 collective-permute-start.3
  27.1 4.3 %collective-permute-start.5 = (bf16[1,128,256]{2,1,0:T(8,128)(2,1)S(1)}, bf16[1,128,256]{2,1,0:T(8,128)(2,1)S(1)}, u32[]{:S(2)}, u32[]{:S(2)}) collective-permute-start(bf16[1,128,256]{2,1,0:T(8,128)(2,1)S(1)} %get-tuple-element.21), channel_id=1, source_target_pairs={{1,16},{2,17},{3,18},{4,19},{5,20},{6,21},{7,22},{8,23},{9,24},{10... | collective-permute-start | bytes 196616 | tf_op jit(solution)/shard_map/ppermute | solution.py:35
  31.4 1.9 collective-permute-start.6
  34.6 4.6 %collective-permute-done.6.refs_7_ = bf16[1,128,256]{2,1,0:T(8,128)(2,1)S(1)} collective-permute-done((bf16[1,128,256]{2,1,0:T(8,128)(2,1)S(1)}, bf16[1,128,256]{2,1,0:T(8,128)(2,1)S(1)}, u32[]{:S(2)}, u32[]{:S(2)}) %collective-permute-start.6) | collective-permute-done | bytes 65568 | tf_op jit(solution)/shard_map/ppermute | solution.py:35
  39.2 2.8 %collective-permute-done.7.refs_8_ = bf16[1,128,256]{2,1,0:T(8,128)(2,1)S(1)} collective-permute-done((bf16[1,128,256]{2,1,0:T(8,128)(2,1)S(1)}, bf16[1,128,256]{2,1,0:T(8,128)(2,1)S(1)}, u32[]{:S(2)}, u32[]{:S(2)}) %collective-permute-start.7) | collective-permute-done | bytes 65568 | tf_op jit(solution)/shard_map/ppermute | solution.py:35
  42.0 2.0 copy-done.2
  44.1 5.1 %shard_map.136.refs_1_ = bf16[4,128,256]{2,1,0:T(8,128)(2,1)S(1)} custom-call(bf16[4,128,256]{2,1,0:T(8,128)(2,1)S(1)} %collective-permute-done.refs_0_, bf16[4,128,256]{2,1,0:T(8,128)(2,1)S(1)} %bitcast.36, bf16[4,128,256]{2,1,0:T(8,128)(2,1)S(1)} %collective-permute-done.1.refs_2_, bf16[1,128,256]{2,1,0:T(8,128)(2,1)S(1)} %collective-permute-done.2.refs_3_, ...), custom_call_target="tpu_custom_call" | custom-call | flops 1811939328 | bytes 3538944 | tf_op jit(solution)/shard_map/pallas_call | solution.py:125
  49.3 5.1 %collective-permute-start.10 = (bf16[1,128,256]{2,1,0:T(8,128)(2,1)S(1)}, bf16[1,128,256]{2,1,0:T(8,128)(2,1)S(1)}, u32[]{:S(2)}, u32[]{:S(2)}) collective-permute-start(bf16[1,128,256]{2,1,0:T(8,128)(2,1)S(1)} %get-tuple-element.20), channel_id=1, source_target_pairs={{0,17},{1,18},{2,19},{3,20},{4,21},{5,22},{6,23},{7,24},{8,25},{9,... | collective-permute-start | bytes 196616 | tf_op jit(solution)/shard_map/ppermute | solution.py:35
  54.4 4.9 %collective-permute-start.11 = (bf16[1,128,256]{2,1,0:T(8,128)(2,1)S(1)}, bf16[1,128,256]{2,1,0:T(8,128)(2,1)S(1)}, u32[]{:S(2)}, u32[]{:S(2)}) collective-permute-start(bf16[1,128,256]{2,1,0:T(8,128)(2,1)S(1)} %get-tuple-element.20), channel_id=1, source_target_pairs={{0,1},{1,2},{2,3},{3,4},{4,5},{5,6},{6,7},{7,8},{8,9},{9,10},{10,1... | collective-permute-start | bytes 196616 | tf_op jit(solution)/shard_map/ppermute | solution.py:35
  59.3 1.3 collective-permute-start.12
  60.6 7.3 %collective-permute-start.8 = (bf16[4,128,256]{2,1,0:T(8,128)(2,1)S(1)}, bf16[4,128,256]{2,1,0:T(8,128)(2,1)S(1)}, u32[]{:S(2)}, u32[]{:S(2)}) collective-permute-start(bf16[4,128,256]{2,1,0:T(8,128)(2,1)S(1)} %shard_map.136.refs_1_), channel_id=1, source_target_pairs={{0,16},{1,17},{2,18},{3,19},{4,20},{5,21},{6,22},{7,23},{8,24},{9,... | collective-permute-start | bytes 786440 | tf_op jit(solution)/shard_map/ppermute | solution.py:35
  69.3 6.0 %collective-permute-start.13 = (bf16[1,128,256]{2,1,0:T(8,128)(2,1)S(1)}, bf16[1,128,256]{2,1,0:T(8,128)(2,1)S(1)}, u32[]{:S(2)}, u32[]{:S(2)}) collective-permute-start(bf16[1,128,256]{2,1,0:T(8,128)(2,1)S(1)} %get-tuple-element.19), channel_id=1, source_target_pairs={{1,16},{2,17},{3,18},{4,19},{5,20},{6,21},{7,22},{8,23},{9,24},{10... | collective-permute-start | bytes 196616 | tf_op jit(solution)/shard_map/ppermute | solution.py:35
  75.3 1.9 collective-permute-start.14
  78.6 1.3 convolution_multiply_fusion.2
  80.2 1.9 collective-permute-done.14.refs_7_
  82.2 3.9 %collective-permute-done.15.refs_8_ = bf16[1,128,256]{2,1,0:T(8,128)(2,1)S(1)} collective-permute-done((bf16[1,128,256]{2,1,0:T(8,128)(2,1)S(1)}, bf16[1,128,256]{2,1,0:T(8,128)(2,1)S(1)}, u32[]{:S(2)}, u32[]{:S(2)}) %collective-permute-start.15) | collective-permute-done | bytes 65568 | tf_op jit(solution)/shard_map/ppermute | solution.py:35
  86.1 5.5 %shard_map.137 = bf16[128,128]{1,0:T(8,128)(2,1)S(1)} custom-call(bf16[4,128,256]{2,1,0:T(8,128)(2,1)S(1)} %collective-permute-done.8.refs_0_, bf16[4,128,256]{2,1,0:T(8,128)(2,1)S(1)} %shard_map.136.refs_1_, bf16[4,128,256]{2,1,0:T(8,128)(2,1)S(1)} %collective-permute-done.9.refs_2_, bf16[1,128,256]{2,1,0:T(8,128)(2,1)S(1)} %collective-permute-done.10.refs_3_, ...), custom_call_target="tpu_custom_call" | custom-call | flops 1811939328 | bytes 3538944 | tf_op jit(solution)/shard_map/pallas_call | solution.py:125
  92.4 17.0 %all_to_all.5.refs_1_.refs_7_ = bf16[16,144,128]{2,1,0:T(8,128)(2,1)S(1)} all-to-all(bf16[16,144,128]{2,1,0:T(8,128)(2,1)S(1)} %broadcast_in_dim.40), channel_id=1, replica_groups=mesh['aa'=8,'ba'=16] {'ba'}, dimensions={0} | all-to-all | bytes 1179648 | tf_op jit(solution)/shard_map/all_to_all | solution.py:290
  109.4 3.5 %collective-permute-start.22 = (bf16[16,144,128]{2,1,0:T(8,128)(2,1)S(1)}, bf16[16,144,128]{2,1,0:T(8,128)(2,1)S(1)}, u32[]{:S(2)}, u32[]{:S(2)}) collective-permute-start(bf16[16,144,128]{2,1,0:T(8,128)(2,1)S(1)} %all_to_all.5.refs_1_.refs_7_), channel_id=1, source_target_pairs={{0,16},{16,32},{32,48},{48,0},{64,80},{80,96},{96,112},{112,64},{1... | collective-permute-start | bytes 1769480 | tf_op jit(solution)/shard_map/ppermute | solution.py:345
  112.9 8.1 %collective-permute-start.20 = (bf16[16,144,128]{2,1,0:T(8,128)(2,1)S(1)}, bf16[16,144,128]{2,1,0:T(8,128)(2,1)S(1)}, u32[]{:S(2)}, u32[]{:S(2)}) collective-permute-start(bf16[16,144,128]{2,1,0:T(8,128)(2,1)S(1)} %all_to_all.5.refs_1_.refs_7_), channel_id=1, source_target_pairs={{0,48},{16,0},{32,16},{48,32},{64,112},{80,64},{96,80},{112,96},{1... | collective-permute-start | bytes 1769480 | tf_op jit(solution)/shard_map/ppermute | solution.py:345
  122.2 3.5 %collective-permute-start.17 = (bf16[16,144,128]{2,1,0:T(8,128)(2,1)S(1)}, bf16[16,144,128]{2,1,0:T(8,128)(2,1)}, u32[]{:S(2)}, u32[]{:S(2)}) collective-permute-start(bf16[16,144,128]{2,1,0:T(8,128)(2,1)S(1)} %all_to_all.5.refs_1_.refs_7_), channel_id=1, source_target_pairs={{0,80},{16,96},{32,112},{48,64},{64,16},{80,32},{96,48},{112,0},{1... | collective-permute-start | bytes 1769480 | tf_op jit(solution)/shard_map/ppermute | solution.py:345
  125.7 1.7 slice-done
  127.4 1.8 fusion
  129.2 10.4 %shard_map.138 = (f32[1,4096]{1,0:T(1,128)}, f32[32,144,128]{2,1,0:T(8,128)}) custom-call(bf16[32,144,128]{2,1,0:T(8,128)(2,1)} %bitcast.43, bf16[16,144,128]{2,1,0:T(8,128)(2,1)} %copy-done.9), custom_call_target="tpu_custom_call" | custom-call | flops 8589934592 | bytes 4194304 | tf_op jit(solution)/shard_map/pallas_call | solution.py:240
  139.7 18.6 %collective-permute-start.18 = (bf16[16,144,128]{2,1,0:T(8,128)(2,1)S(1)}, bf16[16,144,128]{2,1,0:T(8,128)(2,1)S(1)}, u32[]{:S(2)}, u32[]{:S(2)}) collective-permute-start(bf16[16,144,128]{2,1,0:T(8,128)(2,1)S(1)} %copy-done.10), channel_id=1, source_target_pairs={{0,112},{16,64},{32,80},{48,96},{64,48},{80,0},{96,16},{112,32},{1... | collective-permute-start | bytes 1769480 | tf_op jit(solution)/shard_map/ppermute | solution.py:345
  158.3 10.2 %shard_map.139 = (f32[1,4096]{1,0:T(1,128)}, f32[32,144,128]{2,1,0:T(8,128)}) custom-call(bf16[32,144,128]{2,1,0:T(8,128)(2,1)} %bitcast.44, bf16[16,144,128]{2,1,0:T(8,128)(2,1)} %copy-done.13, f32[1,4096]{1,0:T(1,128)} %get-tuple-element.11.refs_2_, f32[32,144,128]{2,1,0:T(8,128)} %get-tuple-element.12.refs_3_), custom_call_target="tpu_custom_call" | custom-call | flops 8589934592 | bytes 4194304 | tf_op jit(solution)/shard_map/pallas_call | solution.py:240
  168.5 1.8 collective-permute-start.19
  171.2 17.4 %shard_map.140 = (f32[1,4096]{1,0:T(1,128)}, f32[32,144,128]{2,1,0:T(8,128)}) custom-call(bf16[32,144,128]{2,1,0:T(8,128)(2,1)} %bitcast.45, bf16[16,144,128]{2,1,0:T(8,128)(2,1)} %copy-done.14, bf16[16,144,128]{2,1,0:T(8,128)(2,1)} %copy-done.15, f32[1,4096]{1,0:T(1,128)} %get-tuple-element.13.refs_3_, f32[32,144,128]{2,1,0:T(8,128)} %get-tuple-element.14.refs_4_), custom_call_target="tpu_custom_call" | custom-call | flops 17179869184 | bytes 4194304 | tf_op jit(solution)/shard_map/pallas_call | solution.py:240
  189.8 32.6 %shard_map.141 = bf16[32,144,128]{2,1,0:T(8,128)(2,1)} custom-call(bf16[32,144,128]{2,1,0:T(8,128)(2,1)} %bitcast.46, bf16[16,144,128]{2,1,0:T(8,128)(2,1)} %collective-permute-done.16.refs_1_.refs_11_, bf16[16,144,128]{2,1,0:T(8,128)(2,1)} %collective-permute-done.17.refs_2_.refs_12_, bf16[16,144,128]{2,1,0:T(8,128)(2,1)} %copy-done.16, ...), custom_call_target="tpu_custom_call" | custom-call | flops 34359738368 | bytes 4194304 | tf_op jit(solution)/shard_map/pallas_call | solution.py:240
  222.4 2.4 %fusion.13 = f32[128,128]{1,0:T(8,128)} fusion(bf16[32,144,128]{2,1,0:T(8,128)(2,1)} %shard_map.141, bf16[32,144,272]{2,1,0:T(8,128)(2,1)S(1)} %copy-done.8), kind=kOutput, calls=%fused_computation.20 | convolution fusion | flops 150994944 | bytes 2424832 | tf_op jit(solution)/shard_map/dot_general | solution.py:356
  (100 shorter events, 16.1 us)
Async XLA Ops:
  6.5 119.2 %all-gather.2.cloned.1.call-start = ((), (), s32[]{:S(2)}) async-start(), calls=%async_computation.1 | async-start | bytes 3760128 | tf_op jit(solution)/shard_map/all_gather | solution.py:313
  10.2 31.8 %copy-start.5 = (f32[256]{0:T(256)S(1)}, f32[256]{0:T(256)}, u32[]{:S(2)}) copy-start(f32[256]{0:T(256)} %param.16) | copy-start | bytes 3076
  12.0 30.0 %collective-permute-start = (bf16[4,128,256]{2,1,0:T(8,128)(2,1)S(1)}, bf16[4,128,256]{2,1,0:T(8,128)(2,1)S(1)}, u32[]{:S(2)}, u32[]{:S(2)}) collective-permute-start(bf16[4,128,256]{2,1,0:T(8,128)(2,1)S(1)} %bitcast.34), channel_id=1, source_target_pairs={{0,16},{1,17},{2,18},{3,19},{4,20},{5,21},{6,22},{7,23},{8,24},{9,... | collective-permute-start | bytes 786440 | tf_op jit(solution)/shard_map/ppermute | solution.py:35
  16.4 25.6 %collective-permute-start.1 = (bf16[4,128,256]{2,1,0:T(8,128)(2,1)S(1)}, bf16[4,128,256]{2,1,0:T(8,128)(2,1)S(1)}, u32[]{:S(2)}, u32[]{:S(2)}) collective-permute-start(bf16[4,128,256]{2,1,0:T(8,128)(2,1)S(1)} %bitcast.35), channel_id=1, source_target_pairs={{16,0},{17,1},{18,2},{19,3},{20,4},{21,5},{22,6},{23,7},{24,8},{25... | collective-permute-start | bytes 786440 | tf_op jit(solution)/shard_map/ppermute | solution.py:35
  17.7 9.4 %collective-permute-start.2 = (bf16[1,128,256]{2,1,0:T(8,128)(2,1)S(1)}, bf16[1,128,256]{2,1,0:T(8,128)(2,1)S(1)}, u32[]{:S(2)}, u32[]{:S(2)}) collective-permute-start(bf16[1,128,256]{2,1,0:T(8,128)(2,1)S(1)} %get-tuple-element.22), channel_id=1, source_target_pairs={{0,17},{1,18},{2,19},{3,20},{4,21},{5,22},{6,23},{7,24},{8,25},{9,... | collective-permute-start | bytes 196616 | tf_op jit(solution)/shard_map/ppermute | solution.py:35
  23.9 7.5 %collective-permute-start.3 = (bf16[1,128,256]{2,1,0:T(8,128)(2,1)S(1)}, bf16[1,128,256]{2,1,0:T(8,128)(2,1)S(1)}, u32[]{:S(2)}, u32[]{:S(2)}) collective-permute-start(bf16[1,128,256]{2,1,0:T(8,128)(2,1)S(1)} %get-tuple-element.22), channel_id=1, source_target_pairs={{0,1},{1,2},{2,3},{3,4},{4,5},{5,6},{6,7},{7,8},{8,9},{9,10},{10,1... | collective-permute-start | bytes 196616 | tf_op jit(solution)/shard_map/ppermute | solution.py:35
  25.8 7.5 %collective-permute-start.4 = (bf16[1,128,256]{2,1,0:T(8,128)(2,1)S(1)}, bf16[1,128,256]{2,1,0:T(8,128)(2,1)S(1)}, u32[]{:S(2)}, u32[]{:S(2)}) collective-permute-start(bf16[1,128,256]{2,1,0:T(8,128)(2,1)S(1)} %get-tuple-element.22), channel_id=1, source_target_pairs={{16,1},{17,2},{18,3},{19,4},{20,5},{21,6},{22,7},{23,8},{24,9},{25... | collective-permute-start | bytes 196616 | tf_op jit(solution)/shard_map/ppermute | solution.py:35
  27.1 7.5 %collective-permute-start.5 = (bf16[1,128,256]{2,1,0:T(8,128)(2,1)S(1)}, bf16[1,128,256]{2,1,0:T(8,128)(2,1)S(1)}, u32[]{:S(2)}, u32[]{:S(2)}) collective-permute-start(bf16[1,128,256]{2,1,0:T(8,128)(2,1)S(1)} %get-tuple-element.21), channel_id=1, source_target_pairs={{1,16},{2,17},{3,18},{4,19},{5,20},{6,21},{7,22},{8,23},{9,24},{10... | collective-permute-start | bytes 196616 | tf_op jit(solution)/shard_map/ppermute | solution.py:35
  31.4 7.8 %collective-permute-start.6 = (bf16[1,128,256]{2,1,0:T(8,128)(2,1)S(1)}, bf16[1,128,256]{2,1,0:T(8,128)(2,1)S(1)}, u32[]{:S(2)}, u32[]{:S(2)}) collective-permute-start(bf16[1,128,256]{2,1,0:T(8,128)(2,1)S(1)} %get-tuple-element.21), channel_id=1, source_target_pairs={{1,0},{2,1},{3,2},{4,3},{5,4},{6,5},{7,6},{8,7},{9,8},{10,9},{11,1... | collective-permute-start | bytes 196616 | tf_op jit(solution)/shard_map/ppermute | solution.py:35
  33.3 8.7 %collective-permute-start.7 = (bf16[1,128,256]{2,1,0:T(8,128)(2,1)S(1)}, bf16[1,128,256]{2,1,0:T(8,128)(2,1)S(1)}, u32[]{:S(2)}, u32[]{:S(2)}) collective-permute-start(bf16[1,128,256]{2,1,0:T(8,128)(2,1)S(1)} %get-tuple-element.21), channel_id=1, source_target_pairs={{17,0},{18,1},{19,2},{20,3},{21,4},{22,5},{23,6},{24,7},{25,8},{26... | collective-permute-start | bytes 196616 | tf_op jit(solution)/shard_map/ppermute | solution.py:35
  44.1 42.0 %copy-start.3 = (bf16[3,3,3,256,256]{4,3,2,1,0:T(8,128)(2,1)S(1)}, bf16[3,3,3,256,256]{4,3,2,1,0:T(8,128)(2,1)}, u32[]{:S(2)}) copy-start(bf16[3,3,3,256,256]{4,3,2,1,0:T(8,128)(2,1)} %refs_9_.3) | copy-start | bytes 10616836
  49.2 36.9 %copy-start.4 = (bf16[2,2,256,128]{3,2,1,0:T(8,128)(2,1)S(1)}, bf16[2,2,256,128]{3,2,1,0:T(8,128)(2,1)}, u32[]{:S(2)}) copy-start(bf16[2,2,256,128]{3,2,1,0:T(8,128)(2,1)} %refs_11_.1) | copy-start | bytes 786436
  49.2 36.9 %copy-start.6 = (f32[256]{0:T(256)S(1)}, f32[256]{0:T(256)}, u32[]{:S(2)}) copy-start(f32[256]{0:T(256)} %param.18) | copy-start | bytes 3076
  49.2 36.9 %copy-start.7 = (f32[128]{0:T(128)S(1)}, f32[128]{0:T(128)}, u32[]{:S(2)}) copy-start(f32[128]{0:T(128)} %param.20) | copy-start | bytes 1540
  49.3 20.0 %collective-permute-start.10 = (bf16[1,128,256]{2,1,0:T(8,128)(2,1)S(1)}, bf16[1,128,256]{2,1,0:T(8,128)(2,1)S(1)}, u32[]{:S(2)}, u32[]{:S(2)}) collective-permute-start(bf16[1,128,256]{2,1,0:T(8,128)(2,1)S(1)} %get-tuple-element.20), channel_id=1, source_target_pairs={{0,17},{1,18},{2,19},{3,20},{4,21},{5,22},{6,23},{7,24},{8,25},{9,... | collective-permute-start | bytes 196616 | tf_op jit(solution)/shard_map/ppermute | solution.py:35
  54.4 20.9 %collective-permute-start.11 = (bf16[1,128,256]{2,1,0:T(8,128)(2,1)S(1)}, bf16[1,128,256]{2,1,0:T(8,128)(2,1)S(1)}, u32[]{:S(2)}, u32[]{:S(2)}) collective-permute-start(bf16[1,128,256]{2,1,0:T(8,128)(2,1)S(1)} %get-tuple-element.20), channel_id=1, source_target_pairs={{0,1},{1,2},{2,3},{3,4},{4,5},{5,6},{6,7},{7,8},{8,9},{9,10},{10,1... | collective-permute-start | bytes 196616 | tf_op jit(solution)/shard_map/ppermute | solution.py:35
  59.3 17.9 %collective-permute-start.12 = (bf16[1,128,256]{2,1,0:T(8,128)(2,1)S(1)}, bf16[1,128,256]{2,1,0:T(8,128)(2,1)S(1)}, u32[]{:S(2)}, u32[]{:S(2)}) collective-permute-start(bf16[1,128,256]{2,1,0:T(8,128)(2,1)S(1)} %get-tuple-element.20), channel_id=1, source_target_pairs={{16,1},{17,2},{18,3},{19,4},{20,5},{21,6},{22,7},{23,8},{24,9},{25... | collective-permute-start | bytes 196616 | tf_op jit(solution)/shard_map/ppermute | solution.py:35
  60.6 25.5 %collective-permute-start.8 = (bf16[4,128,256]{2,1,0:T(8,128)(2,1)S(1)}, bf16[4,128,256]{2,1,0:T(8,128)(2,1)S(1)}, u32[]{:S(2)}, u32[]{:S(2)}) collective-permute-start(bf16[4,128,256]{2,1,0:T(8,128)(2,1)S(1)} %shard_map.136.refs_1_), channel_id=1, source_target_pairs={{0,16},{1,17},{2,18},{3,19},{4,20},{5,21},{6,22},{7,23},{8,24},{9,... | collective-permute-start | bytes 786440 | tf_op jit(solution)/shard_map/ppermute | solution.py:35
  68.0 18.1 %collective-permute-start.9 = (bf16[4,128,256]{2,1,0:T(8,128)(2,1)S(1)}, bf16[4,128,256]{2,1,0:T(8,128)(2,1)S(1)}, u32[]{:S(2)}, u32[]{:S(2)}) collective-permute-start(bf16[4,128,256]{2,1,0:T(8,128)(2,1)S(1)} %shard_map.136.refs_1_), channel_id=1, source_target_pairs={{16,0},{17,1},{18,2},{19,3},{20,4},{21,5},{22,6},{23,7},{24,8},{25... | collective-permute-start | bytes 786440 | tf_op jit(solution)/shard_map/ppermute | solution.py:35
  69.3 10.9 %collective-permute-start.13 = (bf16[1,128,256]{2,1,0:T(8,128)(2,1)S(1)}, bf16[1,128,256]{2,1,0:T(8,128)(2,1)S(1)}, u32[]{:S(2)}, u32[]{:S(2)}) collective-permute-start(bf16[1,128,256]{2,1,0:T(8,128)(2,1)S(1)} %get-tuple-element.19), channel_id=1, source_target_pairs={{1,16},{2,17},{3,18},{4,19},{5,20},{6,21},{7,22},{8,23},{9,24},{10... | collective-permute-start | bytes 196616 | tf_op jit(solution)/shard_map/ppermute | solution.py:35
  75.3 6.8 %collective-permute-start.14 = (bf16[1,128,256]{2,1,0:T(8,128)(2,1)S(1)}, bf16[1,128,256]{2,1,0:T(8,128)(2,1)S(1)}, u32[]{:S(2)}, u32[]{:S(2)}) collective-permute-start(bf16[1,128,256]{2,1,0:T(8,128)(2,1)S(1)} %get-tuple-element.19), channel_id=1, source_target_pairs={{1,0},{2,1},{3,2},{4,3},{5,4},{6,5},{7,6},{8,7},{9,8},{10,9},{11,1... | collective-permute-start | bytes 196616 | tf_op jit(solution)/shard_map/ppermute | solution.py:35
  77.3 8.8 %collective-permute-start.15 = (bf16[1,128,256]{2,1,0:T(8,128)(2,1)S(1)}, bf16[1,128,256]{2,1,0:T(8,128)(2,1)S(1)}, u32[]{:S(2)}, u32[]{:S(2)}) collective-permute-start(bf16[1,128,256]{2,1,0:T(8,128)(2,1)S(1)} %get-tuple-element.19), channel_id=1, source_target_pairs={{17,0},{18,1},{19,2},{20,3},{21,4},{22,5},{23,6},{24,7},{25,8},{26... | collective-permute-start | bytes 196616 | tf_op jit(solution)/shard_map/ppermute | solution.py:35
  109.4 16.3 %copy-start.9 = (bf16[16,144,128]{2,1,0:T(8,128)(2,1)}, bf16[16,144,128]{2,1,0:T(8,128)(2,1)S(1)}, u32[]{:S(2)}) copy-start(bf16[16,144,128]{2,1,0:T(8,128)(2,1)S(1)} %all_to_all.5.refs_1_.refs_7_) | copy-start | bytes 1769476
  109.4 30.3 %collective-permute-start.22 = (bf16[16,144,128]{2,1,0:T(8,128)(2,1)S(1)}, bf16[16,144,128]{2,1,0:T(8,128)(2,1)S(1)}, u32[]{:S(2)}, u32[]{:S(2)}) collective-permute-start(bf16[16,144,128]{2,1,0:T(8,128)(2,1)S(1)} %all_to_all.5.refs_1_.refs_7_), channel_id=1, source_target_pairs={{0,16},{16,32},{32,48},{48,0},{64,80},{80,96},{96,112},{112,64},{1... | collective-permute-start | bytes 1769480 | tf_op jit(solution)/shard_map/ppermute | solution.py:345
  112.9 55.6 %collective-permute-start.20 = (bf16[16,144,128]{2,1,0:T(8,128)(2,1)S(1)}, bf16[16,144,128]{2,1,0:T(8,128)(2,1)S(1)}, u32[]{:S(2)}, u32[]{:S(2)}) collective-permute-start(bf16[16,144,128]{2,1,0:T(8,128)(2,1)S(1)} %all_to_all.5.refs_1_.refs_7_), channel_id=1, source_target_pairs={{0,48},{16,0},{32,16},{48,32},{64,112},{80,64},{96,80},{112,96},{1... | collective-permute-start | bytes 1769480 | tf_op jit(solution)/shard_map/ppermute | solution.py:345
  121.0 49.3 %collective-permute-start.21 = (bf16[16,144,128]{2,1,0:T(8,128)(2,1)S(1)}, bf16[16,144,128]{2,1,0:T(8,128)(2,1)S(1)}, u32[]{:S(2)}, u32[]{:S(2)}) collective-permute-start(bf16[16,144,128]{2,1,0:T(8,128)(2,1)S(1)} %all_to_all.5.refs_1_.refs_7_), channel_id=1, source_target_pairs={{0,64},{16,80},{32,96},{48,112},{64,0},{80,16},{96,32},{112,48},{1... | collective-permute-start | bytes 1769480 | tf_op jit(solution)/shard_map/ppermute | solution.py:345
  121.0 67.6 %collective-permute-start.16 = (bf16[16,144,128]{2,1,0:T(8,128)(2,1)S(1)}, bf16[16,144,128]{2,1,0:T(8,128)(2,1)}, u32[]{:S(2)}, u32[]{:S(2)}) collective-permute-start(bf16[16,144,128]{2,1,0:T(8,128)(2,1)S(1)} %all_to_all.5.refs_1_.refs_7_), channel_id=1, source_target_pairs={{0,32},{16,48},{32,0},{48,16},{64,96},{80,112},{96,64},{112,80},{1... | collective-permute-start | bytes 1769480 | tf_op jit(solution)/shard_map/ppermute | solution.py:345
  122.2 66.4 %collective-permute-start.17 = (bf16[16,144,128]{2,1,0:T(8,128)(2,1)S(1)}, bf16[16,144,128]{2,1,0:T(8,128)(2,1)}, u32[]{:S(2)}, u32[]{:S(2)}) collective-permute-start(bf16[16,144,128]{2,1,0:T(8,128)(2,1)S(1)} %all_to_all.5.refs_1_.refs_7_), channel_id=1, source_target_pairs={{0,80},{16,96},{32,112},{48,64},{64,16},{80,32},{96,48},{112,0},{1... | collective-permute-start | bytes 1769480 | tf_op jit(solution)/shard_map/ppermute | solution.py:345
  139.7 18.6 %copy-start.13 = (bf16[16,144,128]{2,1,0:T(8,128)(2,1)}, bf16[16,144,128]{2,1,0:T(8,128)(2,1)S(1)}, u32[]{:S(2)}) copy-start(bf16[16,144,128]{2,1,0:T(8,128)(2,1)S(1)} %collective-permute-done.22.refs_1_.refs_8_) | copy-start | bytes 1769476
  139.7 49.0 %collective-permute-start.18 = (bf16[16,144,128]{2,1,0:T(8,128)(2,1)S(1)}, bf16[16,144,128]{2,1,0:T(8,128)(2,1)S(1)}, u32[]{:S(2)}, u32[]{:S(2)}) collective-permute-start(bf16[16,144,128]{2,1,0:T(8,128)(2,1)S(1)} %copy-done.10), channel_id=1, source_target_pairs={{0,112},{16,64},{32,80},{48,96},{64,48},{80,0},{96,16},{112,32},{1... | collective-permute-start | bytes 1769480 | tf_op jit(solution)/shard_map/ppermute | solution.py:345
  168.5 20.2 %collective-permute-start.19 = (bf16[16,144,128]{2,1,0:T(8,128)(2,1)S(1)}, bf16[16,144,128]{2,1,0:T(8,128)(2,1)S(1)}, u32[]{:S(2)}, u32[]{:S(2)}) collective-permute-start(bf16[16,144,128]{2,1,0:T(8,128)(2,1)S(1)} %copy-done.10), channel_id=1, source_target_pairs={{0,96},{16,112},{32,64},{48,80},{64,32},{80,48},{96,0},{112,16},{1... | collective-permute-start | bytes 1769480 | tf_op jit(solution)/shard_map/ppermute | solution.py:345
  189.8 32.6 %copy-start.8 = (bf16[32,144,272]{2,1,0:T(8,128)(2,1)S(1)}, bf16[32,144,272]{2,1,0:T(8,128)(2,1)}, u32[]{:S(2)}) copy-start(bf16[32,144,272]{2,1,0:T(8,128)(2,1)} %all-gather.2.cloned.1.call-done) | copy-start | bytes 7520260
  (14 other events, 31.5 us)
Sparse Core Ops, SparseCore 0:
  12.1 41.0 all-gather.1

commit v2 on v1

--- a/solution.py
+++ b/solution.py
@@ -23,23 +23,18 @@
     return 0.5 * x * (1.0 + lax.erf(x * (1.0 / math.sqrt(2.0))))
 
 
-def neighbours(block, row_axis):
+def neighbours(block):
     na, nb = lax.axis_size("aa"), lax.axis_size("ba")
 
-    def shift(x, da, db):
-        pairs = []
-        for a in range(na):
-            for b in range(nb):
-                if 0 <= a + da < na and 0 <= b + db < nb:
-                    pairs.append((a * nb + b, (a + da) * nb + b + db))
-        return lax.ppermute(x, ("aa", "ba"), pairs)
-
-    top, bottom = block[:1], block[-1:]
-    before = shift(block, 1, 0)
-    after = shift(block, -1, 0)
-    ups = [shift(bottom, da, 1) for da in (1, 0, -1)]
-    downs = [shift(top, da, -1) for da in (1, 0, -1)]
-    return (before, block, after, *ups, *downs)
+    def shift(x, axis, count, by):
+        pairs = [(i, i + by) for i in range(count) if 0 <= i + by < count]
+        return lax.ppermute(x, axis, pairs)
+
+    before = shift(block, "aa", na, 1)
+    after = shift(block, "aa", na, -1)
+    up = shift(jnp.stack([before[-1], block[-1], after[-1]]), "ba", nb, 1)
+    down = shift(jnp.stack([before[0], block[0], after[0]]), "ba", nb, -1)
+    return (before, block, after, up, down)
 
 
 def conv_taps(refs, w_ref, pad_ref, acc_ref):
@@ -49,10 +44,10 @@
     @pl.when(step == 0)
     def _():
         for t in range(3):
-            pad_ref[t, 0:width] = refs[3 + t][0]
+            pad_ref[t, 0:width] = refs[3][t]
             for r in range(rows):
                 pad_ref[t, (r + 1) * width : (r + 2) * width] = refs[t][r]
-            pad_ref[t, (rows + 1) * width : (rows + 2) * width] = refs[6 + t][0]
+            pad_ref[t, (rows + 1) * width : (rows + 2) * width] = refs[4][t]
 
     for w in range(3):
         total = jnp.dot(pad_ref[step, 0 : rows * width], w_ref[0, 0, w], preferred_element_type=F32)
@@ -81,7 +76,7 @@
 
 
 def first_kernel(*refs):
-    halo, (w_ref, bias_ref, out_ref, pad_ref, acc_ref) = refs[:9], refs[9:]
+    halo, (w_ref, bias_ref, out_ref, pad_ref, acc_ref) = refs[:5], refs[5:]
     conv_taps(halo, w_ref, pad_ref, acc_ref)
 
     @pl.when(pl.program_id(0) == 2)
@@ -91,7 +86,7 @@
 
 
 def second_kernel(*refs):
-    halo, (w_ref, bias_ref, pw_ref, pb_ref, out_ref, pad_ref, acc_ref) = refs[:9], refs[9:]
+    halo, (w_ref, bias_ref, pw_ref, pb_ref, out_ref, pad_ref, acc_ref) = refs[:5], refs[5:]
     conv_taps(halo, w_ref, pad_ref, acc_ref)
 
     @pl.when(pl.program_id(0) == 2)
@@ -125,7 +120,7 @@
     return pl.pallas_call(
         kernel,
         grid=(3,),
-        in_specs=whole * 9
+        in_specs=whole * 5
         + [pl.BlockSpec((1, 3, 3, chans, chans), lambda i: (i, 0, 0, 0, 0))]
         + whole * len(extras),
         out_specs=pl.BlockSpec(memory_space=pltpu.VMEM),
@@ -221,7 +216,7 @@
     whole = pl.BlockSpec(memory_space=pltpu.VMEM)
     args, specs = [queries, *blocks], [per_q] + [whole] * len(blocks)
     if not start:
-        args += state
+        args += list(state)
         specs += [per_m, per_q]
     scratch = []
     if finish:
@@ -310,12 +305,17 @@
     gram, maps = projections(
         embed_weight, embed_bias, norm_gain, w_query, w_key, w_value, w_velocity
     )
-    maps = lax.all_gather(maps, "ba", axis=0, tiled=True)
+    peers = lax.axis_size("ba")
+    far_bit = peers // 2
+    while far_bit:
+        pairs = [(i, i ^ far_bit) for i in range(peers)]
+        maps = jnp.concatenate([maps, lax.ppermute(maps, "ba", pairs)], axis=0)
+        far_bit //= 2
     n_heads = maps.shape[0]
 
-    halo = neighbours(feats[0], 0)
+    halo = neighbours(feats[0])
     first = conv_call(first_kernel, halo, conv_one, [bias_one[None]], (rows, width, chans))
-    halo = neighbours(first, 0)
+    halo = neighbours(first)
     tokens = rows * width // 4
     latents = conv_call(
         second_kernel,
@@ -335,23 +335,30 @@
     block = copy_for_each(own, "ba")
     count = lax.axis_size("aa")
     inner = count // 2
-    blocks = [block]
-    for dx, dz in ((0, 1), (0, 3), (1, 0), (0, 2), (1, 1), (1, 3), (1, 2)):
+    def send(source, dx, dz):
         pairs = [
             (x * inner + z, (x + dx) % 2 * inner + (z + dz) % inner)
             for x in range(2)
             for z in range(inner)
         ]
-        blocks.append(lax.ppermute(block, "aa", pairs))
+        return lax.ppermute(source, "aa", pairs)
+
+    near = [send(block, 0, 1), send(block, 0, 3), send(block, 1, 0)]
 
     forms = maps[:, :, TILE:].reshape(n_heads * DEPTH, DEPTH)
     queries = jnp.dot(forms, columns.astype(BF), preferred_element_type=F32) * rstd
     queries = queries.astype(BF).reshape(n_heads, DEPTH, tokens)
 
-    state = attend_call(queries, blocks[:1], None, None, 8)
-    state = attend_call(queries, blocks[1:2], state, None, 8)
-    state = attend_call(queries, blocks[2:4], state, None, 8)
-    attended = attend_call(queries, blocks[4:], state, blocks, 8)
+    state = attend_call(queries, [block], None, None, 8)
+    block, near, state = lax.optimization_barrier((block, near, state))
+    far = [
+        send(block, 1, 2),
+        send(near[0], 0, 1),
+        send(near[0], 1, 0),
+        send(near[2], 0, 3),
+    ]
+    state = attend_call(queries, near, state, None, 8)
+    attended = attend_call(queries, far, state, [block, *near, *far], 8)
     outs = maps[:, :, :TILE].reshape(n_heads * DEPTH, TILE)
     return lax.dot_general(
         attended.reshape(n_heads * DEPTH, tokens), outs, TN, preferred_element_type=F32

time: 236 us -> 184 us (0.78)
  starting transfers between devices: 88.4 us -> 52.7 us
  blocking collectives: 17 us -> 0 us
  between operations: 14 us -> 0.56 us
  waiting for transfers between devices: 13.3 us -> 26 us
  Pallas kernels: 81.3 us -> 78.1 us
  local copies, waits for them, and re-layouts: 7.5 us -> 10.2 us
  other arithmetic: 2.61 us -> 5.08 us
    ppermute x23 -> x19, starting transfers between devices: 88.4 us -> 47.2 us  [the longest x8 25.2 us: shift(): return lax.ppermute(x, axis, pairs)]
    all_to_all x1 -> x0, blocking collectives: 17 us -> none  [copy_for_each(): return lax.all_to_all(copies, axis, split_axis=0, concat_axis=0, tiled=True)]
    all_to_all x0 -> x1, waiting for transfers between devices: none -> 8.02 us  [copy_for_each(): return lax.all_to_all(copies, axis, split_axis=0, concat_axis=0, tiled=True)]
    all_to_all x0 -> x1, starting transfers between devices: none -> 5.52 us  [copy_for_each(): return lax.all_to_all(copies, axis, split_axis=0, concat_axis=0, tiled=True)]
    ppermute x23 -> x19, waiting for transfers between devices: 13.3 us -> 18 us  [the longest x8 17.7 us: shift(): return lax.ppermute(x, axis, pairs)]
    pallas_call x4 -> x3, Pallas kernels: 70.7 us -> 67.4 us  [attend_call(): pl.pallas_call(functools.partial(attend_kernel, len(blocks), start, finis...]
    concatenate x0 -> x1, local copies, waits for them, and re-layouts: none -> 2.86 us  [on_device(): maps = jnp.concatenate([maps, lax.ppermute(maps, 'ba', pairs)], axis=0)]
    unnamed x42 -> x47, local copies, waits for them, and re-layouts: 5.08 us -> 3.84 us
  transfers between devices with their start and end apart: 24 -> 20, of which waited for: 4 -> 7; matrix products, arithmetic and copies ran while one was open for 2% -> 10% of each run, Pallas kernels for 21% -> 25%
where the time goes in v2:
time: 184 us; the launch traced here: 180 us
  Pallas kernels  78.1 us (42%)
  starting transfers between devices  52.7 us (29%)
  waiting for transfers between devices  26 us (14%)
  local copies, waits for them, and re-layouts  10.2 us (6%)
  matrix products  7.86 us (4%)
  other arithmetic  5.08 us (3%)
    pallas_call x3, Pallas kernels, attend_call(): pl.pallas_call(functools.partial(attend_kernel, len(blocks), start, finis...  67.4 us
    ppermute x8, starting transfers between devices, shift(): return lax.ppermute(x, axis, pairs)  25.2 us
    ppermute x7, starting transfers between devices, send(): return lax.ppermute(source, 'aa', pairs)  17.7 us
    ppermute x8, waiting for transfers between devices, shift(): return lax.ppermute(x, axis, pairs)  17.7 us
    pallas_call x2, Pallas kernels, conv_call(): pl.pallas_call(kernel, grid=(3,), in_specs=whole * 5 + [pl.BlockSpec((1,...  10.7 us
    all_to_all x1, waiting for transfers between devices, copy_for_each(): return lax.all_to_all(copies, axis, split_axis=0, concat_axis=0, tiled=True)  8.02 us
    all_to_all x1, starting transfers between devices, copy_for_each(): return lax.all_to_all(copies, axis, split_axis=0, concat_axis=0, tiled=True)  5.52 us
    ppermute x4, starting transfers between devices, on_device(): maps = jnp.concatenate([maps, lax.ppermute(maps, 'ba', pairs)], axis=0)  4.32 us
  transfers between devices with their start and end apart: 20, of which 7 were waited for; matrix products, arithmetic and copies ran while one was open for 10% of the time, Pallas kernels for 25%

profile of v2, /device:TPU:1, one launch (start us, length us, event | category | flops | bytes accessed | tf_op | source)
XLA Modules:
  0.0 180.4 jit_solution(10439953052536382110)
XLA Ops:
  0.0 1.4 collective-permute-start.5
  1.4 5.0 %collective-permute-start.4 = (bf16[4,128,256]{2,1,0:T(8,128)(2,1)}, bf16[4,128,256]{2,1,0:T(8,128)(2,1)S(1)}, u32[]{:S(2)}, u32[]{:S(2)}) collective-permute-start(bf16[4,128,256]{2,1,0:T(8,128)(2,1)} %bitcast.35), channel_id=1, source_target_pairs={{0,16},{16,32},{32,48},{48,64},{64,80},{80,96},{96,112},{1,17},{17... | collective-permute-start | bytes 786440 | tf_op jit(solution)/shard_map/ppermute | solution.py:31
  6.5 1.1 convert_element_type.22
  7.7 1.0 fusion.27
  11.7 1.2 collective-permute-start
  13.1 4.4 %collective-permute-start.6 = (bf16[3,128,256]{2,1,0:T(8,128)(2,1)S(1)}, bf16[3,128,256]{2,1,0:T(8,128)(2,1)S(1)}, u32[]{:S(2)}, u32[]{:S(2)}) collective-permute-start(bf16[3,128,256]{2,1,0:T(8,128)(2,1)S(1)} %pad_maximum_fusion.4), channel_id=1, source_target_pairs={{0,1},{1,2},{2,3},{3,4},{4,5},{5,6},{6,7},{7,8},{8,9},{9,10},{10,1... | collective-permute-start | bytes 589832 | tf_op jit(solution)/shard_map/ppermute | solution.py:31
  17.5 1.9 %collective-permute-start.7 = (bf16[3,128,256]{2,1,0:T(8,128)(2,1)S(1)}, bf16[3,128,256]{2,1,0:T(8,128)(2,1)S(1)}, u32[]{:S(2)}, u32[]{:S(2)}) collective-permute-start(bf16[3,128,256]{2,1,0:T(8,128)(2,1)S(1)} %pad_maximum_fusion.5), channel_id=1, source_target_pairs={{1,0},{2,1},{3,2},{4,3},{5,4},{6,5},{7,6},{8,7},{9,8},{10,9},{11,1... | collective-permute-start | bytes 589832 | tf_op jit(solution)/shard_map/ppermute | solution.py:31
  19.5 2.7 %collective-permute-start.1 = (bf16[4,144,272]{2,1,0:T(8,128)(2,1)S(1)}, bf16[4,144,272]{2,1,0:T(8,128)(2,1)S(1)}, u32[]{:S(2)}, u32[]{:S(2)}) collective-permute-start(bf16[4,144,272]{2,1,0:T(8,128)(2,1)S(1)} %pad_maximum_fusion.2), channel_id=1, source_target_pairs={{0,4},{1,5},{2,6},{3,7},{4,0},{5,1},{6,2},{7,3},{8,12},{9,13},{10,... | collective-permute-start | bytes 940040 | tf_op jit(solution)/shard_map/ppermute | solution.py:312
  22.2 4.4 %collective-permute-done.7.refs_4_ = bf16[3,128,256]{2,1,0:T(8,128)(2,1)S(1)} collective-permute-done((bf16[3,128,256]{2,1,0:T(8,128)(2,1)S(1)}, bf16[3,128,256]{2,1,0:T(8,128)(2,1)S(1)}, u32[]{:S(2)}, u32[]{:S(2)}) %collective-permute-start.7) | collective-permute-done | bytes 196640 | tf_op jit(solution)/shard_map/ppermute | solution.py:31
  26.6 5.2 %shard_map.136.refs_1_ = bf16[4,128,256]{2,1,0:T(8,128)(2,1)S(1)} custom-call(bf16[4,128,256]{2,1,0:T(8,128)(2,1)S(1)} %collective-permute-done.4.refs_0_, bf16[4,128,256]{2,1,0:T(8,128)(2,1)S(1)} %bitcast.36, bf16[4,128,256]{2,1,0:T(8,128)(2,1)S(1)} %collective-permute-done.5.refs_2_, bf16[3,128,256]{2,1,0:T(8,128)(2,1)S(1)} %collective-permute-done.6.refs_3_, ...), custom_call_target="tpu_custom_call" | custom-call | flops 1811939328 | bytes 3538944 | tf_op jit(solution)/shard_map/pallas_call | solution.py:120
  31.8 1.3 collective-permute-start.9
  33.1 4.1 %collective-permute-start.8 = (bf16[4,128,256]{2,1,0:T(8,128)(2,1)S(1)}, bf16[4,128,256]{2,1,0:T(8,128)(2,1)S(1)}, u32[]{:S(2)}, u32[]{:S(2)}) collective-permute-start(bf16[4,128,256]{2,1,0:T(8,128)(2,1)S(1)} %shard_map.136.refs_1_), channel_id=1, source_target_pairs={{0,16},{16,32},{32,48},{48,64},{64,80},{80,96},{96,112},{1,17},{17... | collective-permute-start | bytes 786440 | tf_op jit(solution)/shard_map/ppermute | solution.py:31
  37.8 1.5 collective-permute-done.9.refs_2_
  39.3 1.4 collective-permute-done.8.refs_0_
  40.7 5.1 %collective-permute-start.10 = (bf16[3,128,256]{2,1,0:T(8,128)(2,1)S(1)}, bf16[3,128,256]{2,1,0:T(8,128)(2,1)S(1)}, u32[]{:S(2)}, u32[]{:S(2)}) collective-permute-start(bf16[3,128,256]{2,1,0:T(8,128)(2,1)S(1)} %pad_maximum_fusion.6), channel_id=1, source_target_pairs={{0,1},{1,2},{2,3},{3,4},{4,5},{5,6},{6,7},{7,8},{8,9},{9,10},{10,1... | collective-permute-start | bytes 589832 | tf_op jit(solution)/shard_map/ppermute | solution.py:31
  45.8 1.9 %collective-permute-start.11 = (bf16[3,128,256]{2,1,0:T(8,128)(2,1)S(1)}, bf16[3,128,256]{2,1,0:T(8,128)(2,1)S(1)}, u32[]{:S(2)}, u32[]{:S(2)}) collective-permute-start(bf16[3,128,256]{2,1,0:T(8,128)(2,1)S(1)} %pad_maximum_fusion.7), channel_id=1, source_target_pairs={{1,0},{2,1},{3,2},{4,3},{5,4},{6,5},{7,6},{8,7},{9,8},{10,9},{11,1... | collective-permute-start | bytes 589832 | tf_op jit(solution)/shard_map/ppermute | solution.py:31
  47.8 1.3 convolution_multiply_fusion.2
  49.4 10.0 %collective-permute-done.10.refs_3_ = bf16[3,128,256]{2,1,0:T(8,128)(2,1)S(1)} collective-permute-done((bf16[3,128,256]{2,1,0:T(8,128)(2,1)S(1)}, bf16[3,128,256]{2,1,0:T(8,128)(2,1)S(1)}, u32[]{:S(2)}, u32[]{:S(2)}) %collective-permute-start.10) | collective-permute-done | bytes 196640 | tf_op jit(solution)/shard_map/ppermute | solution.py:31
  59.8 5.5 %shard_map.137 = bf16[128,128]{1,0:T(8,128)(2,1)S(1)} custom-call(bf16[4,128,256]{2,1,0:T(8,128)(2,1)S(1)} %collective-permute-done.8.refs_0_, bf16[4,128,256]{2,1,0:T(8,128)(2,1)S(1)} %shard_map.136.refs_1_, bf16[4,128,256]{2,1,0:T(8,128)(2,1)S(1)} %collective-permute-done.9.refs_2_, bf16[3,128,256]{2,1,0:T(8,128)(2,1)S(1)} %collective-permute-done.10.refs_3_, ...), custom_call_target="tpu_custom_call" | custom-call | flops 1811939328 | bytes 3538944 | tf_op jit(solution)/shard_map/pallas_call | solution.py:120
  65.7 1.4 pad_maximum_fusion
  68.4 5.5 %all-to-all-start = ((bf16[16,144,128]{2,1,0:T(8,128)(2,1)}), bf16[16,144,128]{2,1,0:T(8,128)(2,1)S(1)}, u32[]{:S(2)}, u32[]{:S(2)}) async-start(bf16[16,144,128]{2,1,0:T(8,128)(2,1)} %broadcast_in_dim.40), calls=%async_computation | async-start | bytes 1179648 | tf_op jit(solution)/shard_map/all_to_all | solution.py:285
  76.4 8.0 %all-to-all-done.refs_1_.refs_7_ = bf16[16,144,128]{2,1,0:T(8,128)(2,1)S(1)} async-done(((bf16[16,144,128]{2,1,0:T(8,128)(2,1)}), bf16[16,144,128]{2,1,0:T(8,128)(2,1)S(1)}, u32[]{:S(2)}, u32[]{:S(2)}) %all-to-all-start) | async-done | bytes 589856 | tf_op jit(solution)/shard_map/all_to_all | solution.py:285
  84.4 10.5 %collective-permute-start.14 = (bf16[16,144,128]{2,1,0:T(8,128)(2,1)S(1)}, bf16[16,144,128]{2,1,0:T(8,128)(2,1)S(1)}, u32[]{:S(2)}, u32[]{:S(2)}) collective-permute-start(bf16[16,144,128]{2,1,0:T(8,128)(2,1)S(1)} %all-to-all-done.refs_1_.refs_7_), channel_id=1, source_target_pairs={{0,64},{16,80},{32,96},{48,112},{64,0},{80,16},{96,32},{112,48},{1... | collective-permute-start | bytes 1769480 | tf_op jit(solution)/shard_map/ppermute | solution.py:344
  96.4 2.9 %constant_dynamic-update-slice_fusion = bf16[32,144,272]{2,1,0:T(8,128)(2,1)} fusion(bf16[32,144,272]{2,1,0:T(8,128)(2,1)} %constant_dynamic-update-slice_fusion.1, bf16[16,144,272]{2,1,0:T(8,128)(2,1)} %collective-permute-done.3), kind=kLoop, calls=%fused_computation.46 | loop fusion | bytes 3538944 | tf_op jit(solution)/shard_map/concatenate | solution.py:312
  99.3 1.8 %slice.94 = bf16[32,144,144]{2,1,0:T(8,128)(2,1)S(1)} slice(bf16[32,144,272]{2,1,0:T(8,128)(2,1)} %constant_dynamic-update-slice_fusion), slice={[0:32], [0:144], [128:272]} | slice | bytes 2654208 | tf_op jit(solution)/shard_map/slice | solution.py:348
  101.1 1.8 %fusion = bf16[4608,128]{1,0:T(8,128)(2,1)} fusion(bf16[4608,144]{1,0:T(8,128)(2,1)S(1)} %bitcast.40, f32[128]{0:T(128)S(1)} %add_rsqrt_fusion, f32[128,128]{0,1:T(8,128)S(1)} %convert_bitcast_fusion, f32[144]{0:T(256)S(1)} %pad.6.clone, f32[144]{0:T(256)S(1)} %pad.5.clone, f32[144]{0:T(256)S(1)} %pad.4.clone), kind=kOutput, calls=%fused_computation.1 | convolution fusion | flops 171196416 | bytes 2574528 | tf_op jit(solution)/shard_map/dot_general | solution.py:349
  102.9 10.5 %shard_map.138 = (f32[1,4096]{1,0:T(1,128)}, f32[32,144,128]{2,1,0:T(8,128)}) custom-call(bf16[32,144,128]{2,1,0:T(8,128)(2,1)} %bitcast.43, bf16[16,144,128]{2,1,0:T(8,128)(2,1)} %copy-done.8), custom_call_target="tpu_custom_call" | custom-call | flops 8589934592 | bytes 4194304 | tf_op jit(solution)/shard_map/pallas_call | solution.py:235
  113.5 2.0 %collective-permute-start.17 = (bf16[16,144,128]{2,1,0:T(8,128)(2,1)S(1)}, bf16[16,144,128]{2,1,0:T(8,128)(2,1)S(1)}, u32[]{:S(2)}, u32[]{:S(2)}) collective-permute-start(bf16[16,144,128]{2,1,0:T(8,128)(2,1)S(1)} %collective-permute-done.12.refs_1_.refs_8_), channel_id=1, source_target_pairs={{0,64},{16,80},{32,96},{48,112},{64,0},{80,16},{96,32},{112,48},{1... | collective-permute-start | bytes 1769480 | tf_op jit(solution)/shard_map/ppermute | solution.py:344
  115.5 3.7 %collective-permute-start.15 = (bf16[16,144,128]{2,1,0:T(8,128)(2,1)S(1)}, bf16[16,144,128]{2,1,0:T(8,128)(2,1)S(1)}, u32[]{:S(2)}, u32[]{:S(2)}) collective-permute-start(bf16[16,144,128]{2,1,0:T(8,128)(2,1)S(1)} %copy-done.9), channel_id=1, source_target_pairs={{0,96},{16,112},{32,64},{48,80},{64,32},{80,48},{96,0},{112,16},{1... | collective-permute-start | bytes 1769480 | tf_op jit(solution)/shard_map/ppermute | solution.py:344
  119.2 24.6 %shard_map.139 = (f32[1,4096]{1,0:T(1,128)}, f32[32,144,128]{2,1,0:T(8,128)}) custom-call(bf16[32,144,128]{2,1,0:T(8,128)(2,1)} %bitcast.44, bf16[16,144,128]{2,1,0:T(8,128)(2,1)} %copy-done.14, bf16[16,144,128]{2,1,0:T(8,128)(2,1)} %copy-done.13, bf16[16,144,128]{2,1,0:T(8,128)(2,1)} %copy-done.12, f32[1,4096]{1,0:T(1,128)} %get-tuple-element.21.refs_4_, ...), custom_call_target="tpu_custom_call" | custom-call | flops 25769803776 | bytes 4194304 | tf_op jit(solution)/shard_map/pallas_call | solution.py:235
  145.3 32.3 %shard_map.140 = bf16[32,144,128]{2,1,0:T(8,128)(2,1)} custom-call(bf16[32,144,128]{2,1,0:T(8,128)(2,1)} %bitcast.45, bf16[16,144,128]{2,1,0:T(8,128)(2,1)} %copy-done.17, bf16[16,144,128]{2,1,0:T(8,128)(2,1)} %copy-done.16, bf16[16,144,128]{2,1,0:T(8,128)(2,1)} %copy-done.15, bf16[16,144,128]{2,1,0:T(8,128)(2,1)} %copy-done.18, ...), custom_call_target="tpu_custom_call" | custom-call | flops 34359738368 | bytes 4194304 | tf_op jit(solution)/shard_map/pallas_call | solution.py:235
  177.6 2.8 %fusion.13 = f32[128,128]{1,0:T(8,128)} fusion(bf16[32,144,128]{2,1,0:T(8,128)(2,1)} %shard_map.140, bf16[32,144,272]{2,1,0:T(8,128)(2,1)} %constant_dynamic-update-slice_fusion), kind=kOutput, calls=%fused_computation.21 | convolution fusion | flops 150994944 | bytes 2424832 | tf_op jit(solution)/shard_map/dot_general | solution.py:363
  (105 shorter events, 11.6 us)
Async XLA Ops:
  0.0 10.6 %copy-start = (bf16[128,128]{1,0:T(8,128)(2,1)S(1)}, bf16[128,128]{1,0:T(8,128)(2,1)}, u32[]{:S(2)}) copy-start(bf16[128,128]{1,0:T(8,128)(2,1)} %param.27) | copy-start | bytes 98308
  0.0 8.8 %copy-start.10 = (f32[2048]{0:T(1024)S(1)}, f32[2048]{0:T(1024)}, u32[]{:S(2)}) copy-start(f32[2048]{0:T(1024)} %param.22) | copy-start | bytes 24580
  0.0 8.8 %copy-start.11 = (f32[2048]{0:T(1024)S(1)}, f32[2048]{0:T(1024)}, u32[]{:S(2)}) copy-start(f32[2048]{0:T(1024)} %param.23) | copy-start | bytes 24580
  0.0 13.0 %collective-permute-start.5 = (bf16[4,128,256]{2,1,0:T(8,128)(2,1)}, bf16[4,128,256]{2,1,0:T(8,128)(2,1)S(1)}, u32[]{:S(2)}, u32[]{:S(2)}) collective-permute-start(bf16[4,128,256]{2,1,0:T(8,128)(2,1)} %bitcast.34), channel_id=1, source_target_pairs={{16,0},{32,16},{48,32},{64,48},{80,64},{96,80},{112,96},{17,1},{33... | collective-permute-start | bytes 786440 | tf_op jit(solution)/shard_map/ppermute | solution.py:31
  1.4 11.5 %collective-permute-start.4 = (bf16[4,128,256]{2,1,0:T(8,128)(2,1)}, bf16[4,128,256]{2,1,0:T(8,128)(2,1)S(1)}, u32[]{:S(2)}, u32[]{:S(2)}) collective-permute-start(bf16[4,128,256]{2,1,0:T(8,128)(2,1)} %bitcast.35), channel_id=1, source_target_pairs={{0,16},{16,32},{32,48},{48,64},{64,80},{80,96},{96,112},{1,17},{17... | collective-permute-start | bytes 786440 | tf_op jit(solution)/shard_map/ppermute | solution.py:31
  10.1 16.5 %copy-start.2 = (bf16[3,3,3,256,256]{4,3,2,1,0:T(8,128)(2,1)S(1)}, bf16[3,3,3,256,256]{4,3,2,1,0:T(8,128)(2,1)}, u32[]{:S(2)}) copy-start(bf16[3,3,3,256,256]{4,3,2,1,0:T(8,128)(2,1)} %refs_5_.2) | copy-start | bytes 10616836
  10.7 16.0 %copy-start.5 = (f32[256]{0:T(256)S(1)}, f32[256]{0:T(256)}, u32[]{:S(2)}) copy-start(f32[256]{0:T(256)} %param.16) | copy-start | bytes 3076
  11.7 7.7 %collective-permute-start = (bf16[2,144,272]{2,1,0:T(8,128)(2,1)S(1)}, bf16[2,144,272]{2,1,0:T(8,128)(2,1)S(1)}, u32[]{:S(2)}, u32[]{:S(2)}) collective-permute-start(bf16[2,144,272]{2,1,0:T(8,128)(2,1)S(1)} %get-tuple-element.39), channel_id=1, source_target_pairs={{0,8},{1,9},{2,10},{3,11},{4,12},{5,13},{6,14},{7,15},{8,0},{9,1},... | collective-permute-start | bytes 470024 | tf_op jit(solution)/shard_map/ppermute | solution.py:312
  13.1 9.2 %collective-permute-start.6 = (bf16[3,128,256]{2,1,0:T(8,128)(2,1)S(1)}, bf16[3,128,256]{2,1,0:T(8,128)(2,1)S(1)}, u32[]{:S(2)}, u32[]{:S(2)}) collective-permute-start(bf16[3,128,256]{2,1,0:T(8,128)(2,1)S(1)} %pad_maximum_fusion.4), channel_id=1, source_target_pairs={{0,1},{1,2},{2,3},{3,4},{4,5},{5,6},{6,7},{7,8},{8,9},{9,10},{10,1... | collective-permute-start | bytes 589832 | tf_op jit(solution)/shard_map/ppermute | solution.py:31
  17.5 9.1 %collective-permute-start.7 = (bf16[3,128,256]{2,1,0:T(8,128)(2,1)S(1)}, bf16[3,128,256]{2,1,0:T(8,128)(2,1)S(1)}, u32[]{:S(2)}, u32[]{:S(2)}) collective-permute-start(bf16[3,128,256]{2,1,0:T(8,128)(2,1)S(1)} %pad_maximum_fusion.5), channel_id=1, source_target_pairs={{1,0},{2,1},{3,2},{4,3},{5,4},{6,5},{7,6},{8,7},{9,8},{10,9},{11,1... | collective-permute-start | bytes 589832 | tf_op jit(solution)/shard_map/ppermute | solution.py:31
  19.5 17.7 %collective-permute-start.1 = (bf16[4,144,272]{2,1,0:T(8,128)(2,1)S(1)}, bf16[4,144,272]{2,1,0:T(8,128)(2,1)S(1)}, u32[]{:S(2)}, u32[]{:S(2)}) collective-permute-start(bf16[4,144,272]{2,1,0:T(8,128)(2,1)S(1)} %pad_maximum_fusion.2), channel_id=1, source_target_pairs={{0,4},{1,5},{2,6},{3,7},{4,0},{5,1},{6,2},{7,3},{8,12},{9,13},{10,... | collective-permute-start | bytes 940040 | tf_op jit(solution)/shard_map/ppermute | solution.py:312
  31.8 7.5 %collective-permute-start.9 = (bf16[4,128,256]{2,1,0:T(8,128)(2,1)S(1)}, bf16[4,128,256]{2,1,0:T(8,128)(2,1)S(1)}, u32[]{:S(2)}, u32[]{:S(2)}) collective-permute-start(bf16[4,128,256]{2,1,0:T(8,128)(2,1)S(1)} %shard_map.136.refs_1_), channel_id=1, source_target_pairs={{16,0},{32,16},{48,32},{64,48},{80,64},{96,80},{112,96},{17,1},{33... | collective-permute-start | bytes 786440 | tf_op jit(solution)/shard_map/ppermute | solution.py:31
  33.1 7.6 %collective-permute-start.8 = (bf16[4,128,256]{2,1,0:T(8,128)(2,1)S(1)}, bf16[4,128,256]{2,1,0:T(8,128)(2,1)S(1)}, u32[]{:S(2)}, u32[]{:S(2)}) collective-permute-start(bf16[4,128,256]{2,1,0:T(8,128)(2,1)S(1)} %shard_map.136.refs_1_), channel_id=1, source_target_pairs={{0,16},{16,32},{32,48},{48,64},{64,80},{80,96},{96,112},{1,17},{17... | collective-permute-start | bytes 786440 | tf_op jit(solution)/shard_map/ppermute | solution.py:31
  37.2 22.6 %copy-start.3 = (bf16[3,3,3,256,256]{4,3,2,1,0:T(8,128)(2,1)S(1)}, bf16[3,3,3,256,256]{4,3,2,1,0:T(8,128)(2,1)}, u32[]{:S(2)}) copy-start(bf16[3,3,3,256,256]{4,3,2,1,0:T(8,128)(2,1)} %refs_5_.3) | copy-start | bytes 10616836
  37.4 22.4 %copy-start.4 = (bf16[2,2,256,128]{3,2,1,0:T(8,128)(2,1)S(1)}, bf16[2,2,256,128]{3,2,1,0:T(8,128)(2,1)}, u32[]{:S(2)}) copy-start(bf16[2,2,256,128]{3,2,1,0:T(8,128)(2,1)} %refs_7_.1) | copy-start | bytes 786436
  37.4 22.4 %copy-start.6 = (f32[256]{0:T(256)S(1)}, f32[256]{0:T(256)}, u32[]{:S(2)}) copy-start(f32[256]{0:T(256)} %param.18) | copy-start | bytes 3076
  37.4 22.4 %copy-start.7 = (f32[128]{0:T(128)S(1)}, f32[128]{0:T(128)}, u32[]{:S(2)}) copy-start(f32[128]{0:T(128)} %param.20) | copy-start | bytes 1540
  37.4 28.3 %collective-permute-start.2 = (bf16[8,144,272]{2,1,0:T(8,128)(2,1)S(1)}, bf16[8,144,272]{2,1,0:T(8,128)(2,1)S(1)}, u32[]{:S(2)}, u32[]{:S(2)}) collective-permute-start(bf16[8,144,272]{2,1,0:T(8,128)(2,1)S(1)} %pad_maximum_fusion.1), channel_id=1, source_target_pairs={{0,2},{1,3},{2,0},{3,1},{4,6},{5,7},{6,4},{7,5},{8,10},{9,11},{10,... | collective-permute-start | bytes 1880072 | tf_op jit(solution)/shard_map/ppermute | solution.py:312
  40.7 18.6 %collective-permute-start.10 = (bf16[3,128,256]{2,1,0:T(8,128)(2,1)S(1)}, bf16[3,128,256]{2,1,0:T(8,128)(2,1)S(1)}, u32[]{:S(2)}, u32[]{:S(2)}) collective-permute-start(bf16[3,128,256]{2,1,0:T(8,128)(2,1)S(1)} %pad_maximum_fusion.6), channel_id=1, source_target_pairs={{0,1},{1,2},{2,3},{3,4},{4,5},{5,6},{6,7},{7,8},{8,9},{9,10},{10,1... | collective-permute-start | bytes 589832 | tf_op jit(solution)/shard_map/ppermute | solution.py:31
  45.8 14.0 %collective-permute-start.11 = (bf16[3,128,256]{2,1,0:T(8,128)(2,1)S(1)}, bf16[3,128,256]{2,1,0:T(8,128)(2,1)S(1)}, u32[]{:S(2)}, u32[]{:S(2)}) collective-permute-start(bf16[3,128,256]{2,1,0:T(8,128)(2,1)S(1)} %pad_maximum_fusion.7), channel_id=1, source_target_pairs={{1,0},{2,1},{3,2},{4,3},{5,4},{6,5},{7,6},{8,7},{9,8},{10,9},{11,1... | collective-permute-start | bytes 589832 | tf_op jit(solution)/shard_map/ppermute | solution.py:31
  67.2 29.3 %collective-permute-start.3 = (bf16[16,144,272]{2,1,0:T(8,128)(2,1)}, bf16[16,144,272]{2,1,0:T(8,128)(2,1)}, u32[]{:S(2)}, u32[]{:S(2)}) collective-permute-start(bf16[16,144,272]{2,1,0:T(8,128)(2,1)} %pad_maximum_fusion), channel_id=1, source_target_pairs={{0,1},{1,0},{2,3},{3,2},{4,5},{5,4},{6,7},{7,6},{8,9},{9,8},{10,11... | collective-permute-start | bytes 3760136 | tf_op jit(solution)/shard_map/ppermute | solution.py:312
  68.4 16.1 %all-to-all-start = ((bf16[16,144,128]{2,1,0:T(8,128)(2,1)}), bf16[16,144,128]{2,1,0:T(8,128)(2,1)S(1)}, u32[]{:S(2)}, u32[]{:S(2)}) async-start(bf16[16,144,128]{2,1,0:T(8,128)(2,1)} %broadcast_in_dim.40), calls=%async_computation | async-start | bytes 1179648 | tf_op jit(solution)/shard_map/all_to_all | solution.py:285
  84.4 14.8 %copy-start.8 = (bf16[16,144,128]{2,1,0:T(8,128)(2,1)}, bf16[16,144,128]{2,1,0:T(8,128)(2,1)S(1)}, u32[]{:S(2)}) copy-start(bf16[16,144,128]{2,1,0:T(8,128)(2,1)S(1)} %all-to-all-done.refs_1_.refs_7_) | copy-start | bytes 1769476
  84.4 29.0 %collective-permute-start.14 = (bf16[16,144,128]{2,1,0:T(8,128)(2,1)S(1)}, bf16[16,144,128]{2,1,0:T(8,128)(2,1)S(1)}, u32[]{:S(2)}, u32[]{:S(2)}) collective-permute-start(bf16[16,144,128]{2,1,0:T(8,128)(2,1)S(1)} %all-to-all-done.refs_1_.refs_7_), channel_id=1, source_target_pairs={{0,64},{16,80},{32,96},{48,112},{64,0},{80,16},{96,32},{112,48},{1... | collective-permute-start | bytes 1769480 | tf_op jit(solution)/shard_map/ppermute | solution.py:344
  95.0 18.5 %collective-permute-start.13 = (bf16[16,144,128]{2,1,0:T(8,128)(2,1)S(1)}, bf16[16,144,128]{2,1,0:T(8,128)(2,1)S(1)}, u32[]{:S(2)}, u32[]{:S(2)}) collective-permute-start(bf16[16,144,128]{2,1,0:T(8,128)(2,1)S(1)} %all-to-all-done.refs_1_.refs_7_), channel_id=1, source_target_pairs={{0,48},{16,0},{32,16},{48,32},{64,112},{80,64},{96,80},{112,96},{1... | collective-permute-start | bytes 1769480 | tf_op jit(solution)/shard_map/ppermute | solution.py:344
  95.4 18.0 %collective-permute-start.12 = (bf16[16,144,128]{2,1,0:T(8,128)(2,1)S(1)}, bf16[16,144,128]{2,1,0:T(8,128)(2,1)S(1)}, u32[]{:S(2)}, u32[]{:S(2)}) collective-permute-start(bf16[16,144,128]{2,1,0:T(8,128)(2,1)S(1)} %all-to-all-done.refs_1_.refs_7_), channel_id=1, source_target_pairs={{0,16},{16,32},{32,48},{48,0},{64,80},{80,96},{96,112},{112,64},{1... | collective-permute-start | bytes 1769480 | tf_op jit(solution)/shard_map/ppermute | solution.py:344
  102.9 12.6 %copy-start.9 = (bf16[16,144,128]{2,1,0:T(8,128)(2,1)S(1)}, bf16[16,144,128]{2,1,0:T(8,128)(2,1)}, u32[]{:S(2)}) copy-start(bf16[16,144,128]{2,1,0:T(8,128)(2,1)} %copy-done.8) | copy-start | bytes 1769476
  113.4 5.7 %copy-start.12 = (bf16[16,144,128]{2,1,0:T(8,128)(2,1)}, bf16[16,144,128]{2,1,0:T(8,128)(2,1)S(1)}, u32[]{:S(2)}) copy-start(bf16[16,144,128]{2,1,0:T(8,128)(2,1)S(1)} %collective-permute-done.14.refs_3_.refs_10_) | copy-start | bytes 1769476
  113.5 30.6 %collective-permute-start.17 = (bf16[16,144,128]{2,1,0:T(8,128)(2,1)S(1)}, bf16[16,144,128]{2,1,0:T(8,128)(2,1)S(1)}, u32[]{:S(2)}, u32[]{:S(2)}) collective-permute-start(bf16[16,144,128]{2,1,0:T(8,128)(2,1)S(1)} %collective-permute-done.12.refs_1_.refs_8_), channel_id=1, source_target_pairs={{0,64},{16,80},{32,96},{48,112},{64,0},{80,16},{96,32},{112,48},{1... | collective-permute-start | bytes 1769480 | tf_op jit(solution)/shard_map/ppermute | solution.py:344
  115.5 28.6 %collective-permute-start.16 = (bf16[16,144,128]{2,1,0:T(8,128)(2,1)S(1)}, bf16[16,144,128]{2,1,0:T(8,128)(2,1)S(1)}, u32[]{:S(2)}, u32[]{:S(2)}) collective-permute-start(bf16[16,144,128]{2,1,0:T(8,128)(2,1)S(1)} %collective-permute-done.12.refs_1_.refs_8_), channel_id=1, source_target_pairs={{0,16},{16,32},{32,48},{48,0},{64,80},{80,96},{96,112},{112,64},{1... | collective-permute-start | bytes 1769480 | tf_op jit(solution)/shard_map/ppermute | solution.py:344
  115.5 28.3 %collective-permute-start.15 = (bf16[16,144,128]{2,1,0:T(8,128)(2,1)S(1)}, bf16[16,144,128]{2,1,0:T(8,128)(2,1)S(1)}, u32[]{:S(2)}, u32[]{:S(2)}) collective-permute-start(bf16[16,144,128]{2,1,0:T(8,128)(2,1)S(1)} %copy-done.9), channel_id=1, source_target_pairs={{0,96},{16,112},{32,64},{48,80},{64,32},{80,48},{96,0},{112,16},{1... | collective-permute-start | bytes 1769480 | tf_op jit(solution)/shard_map/ppermute | solution.py:344
  119.2 24.9 %collective-permute-start.18 = (bf16[16,144,128]{2,1,0:T(8,128)(2,1)S(1)}, bf16[16,144,128]{2,1,0:T(8,128)(2,1)S(1)}, u32[]{:S(2)}, u32[]{:S(2)}) collective-permute-start(bf16[16,144,128]{2,1,0:T(8,128)(2,1)S(1)} %collective-permute-done.14.refs_3_.refs_10_), channel_id=1, source_target_pairs={{0,48},{16,0},{32,16},{48,32},{64,112},{80,64},{96,80},{112,96},{1... | collective-permute-start | bytes 1769480 | tf_op jit(solution)/shard_map/ppermute | solution.py:344
  (10 other events, 23.0 us)
